TPU v7x, 32 devices: a whole 2x2x4 slice. The times are simulated.
32 devices in a mesh: ctx: 8 (over z, x), tp: 4 (over y, core).
Axes of the slice: x: 2, y: 2, z: 4, core: 2. Of those that a mesh axis runs over, the one named last changes fastest.
Arguments:
- x_resid: bfloat16 [1024, 7168], P('ctx', 'tp'), may hold values from -4.5 to 4.5
- query_nope: bfloat16 [1024, 8192], P('ctx', 'tp'), may hold values from -6 to 6
- query_rope: bfloat16 [1024, 4096], P('ctx', 'tp'), may hold values from -8 to 8
- latent_kv: bfloat16 [512, 1024], P(None, 'ctx'), may hold values from -6 to 6
- key_rope: bfloat16 [64, 1024], P(None, 'ctx'), may hold values from -8 to 8
- absorb_key: bfloat16 [64, 128, 512], P('tp'), may hold values from -0.5 to 0.5
- absorb_value: bfloat16 [64, 512, 128], P('tp'), may hold values from -0.25 to 0.25
- out_proj: bfloat16 [8192, 7168], P('tp'), may hold values from -0.0625 to 0.0625
- norm_gain: bfloat16 [7168], replicated, may hold values from 0.099609375 to 1.8984375
- router: bfloat16 [8, 7168], replicated, may hold values from -0.0625 to 0.0625
- routes: int32 [1024, 4], P('ctx'), may hold values from 0 to 7, all different within a row; in each aligned block of 128 rows (0 to 127, 128 to 255, ...) at most 128 rows name the same one
- gate_proj: bfloat16 [8, 7168, 1024], P('ctx', None, 'tp'), may hold values from -0.0625 to 0.0625
- up_proj: bfloat16 [8, 7168, 1024], P('ctx', None, 'tp'), may hold values from -0.0625 to 0.0625
- down_proj: bfloat16 [8, 1024, 7168], P('ctx', 'tp'), may hold values from -0.1875 to 0.1875
Outputs:
- layer_out: bfloat16 [1024, 7168], P('ctx', 'tp')
Inputs may be any that keep to these rules, and one draw needn't show every extreme that they name: `routes`: each row names 4 different experts; within the rows of one index of ctx no expert is named by more than 128 rows, and that many is reached.
All inputs are finite; a program needn't handle non-finite values.
Results may differ from a plain program's by a relative error of at most 0.033.
Values may be sent and summed in bfloat16 or wider, within the bound.
A program may use at most 192 MiB of HBM per device.

v0:
```python
import jax
import jax.numpy as jnp
from jax import lax
from jax.sharding import PartitionSpec as P

NOPE = 128
ROPE = 64
VDIM = 128
TOP = 4


EPS = 1e-06
ROUTE_SCALE = 2.5
LOW_SCORE = -1e30


def body(
    x_resid,
    query_nope,
    query_rope,
    latent_kv,
    key_rope,
    absorb_key,
    absorb_value,
    out_proj,
    norm_gain,
    router,
    routes,
    gate_proj,
    up_proj,
    down_proj,
):
    row_count = x_resid.shape[0]
    col_width = x_resid.shape[1]
    head_count = absorb_key.shape[0]
    expert_count = lax.axis_size("ctx")
    capacity = 2 * row_count * TOP // expert_count
    col_start = lax.axis_index("tp") * col_width
    query_pos = lax.axis_index("ctx") * row_count + jnp.arange(row_count, dtype=jnp.int32)
    query_lat = jnp.einsum(
        "thn,hnl->thl",
        query_nope.reshape(row_count, head_count, NOPE),
        absorb_key,
        preferred_element_type=jnp.float32,
    ).astype(jnp.bfloat16)
    query_rot = query_rope.reshape(row_count, head_count, ROPE)
    score_scale = (NOPE + ROPE) ** (-0.5)
    running = jnp.full((row_count, head_count), LOW_SCORE, jnp.float32)
    latent = lax.all_gather(latent_kv, "ctx", axis=1, tiled=True)
    rotary = lax.all_gather(key_rope, "ctx", axis=1, tiled=True)
    scores = jnp.einsum("thl,ls->ths", query_lat, latent, preferred_element_type=jnp.float32)
    scores = (
        scores + jnp.einsum("thr,rs->ths", query_rot, rotary, preferred_element_type=jnp.float32)
    ) * score_scale
    key_pos = jnp.arange(latent.shape[1], dtype=jnp.int32)
    allowed = (key_pos[None, :] <= query_pos[:, None])[:, None, :]
    new_max = jnp.maximum(running, jnp.max(jnp.where(allowed, scores, LOW_SCORE), axis=2))
    exp_scores = jnp.where(allowed, jnp.exp(scores - new_max[:, :, None]), 0.0)
    norm_sum = jnp.sum(exp_scores, axis=2)
    weighted = jnp.einsum(
        "ths,ls->thl", exp_scores.astype(jnp.bfloat16), latent, preferred_element_type=jnp.float32
    )
    running, norm_sum, weighted = (new_max, norm_sum, weighted)
    attn_lat = (weighted / norm_sum[:, :, None]).astype(jnp.bfloat16)
    heads_out = jnp.einsum(
        "thl,hlv->thv", attn_lat, absorb_value, preferred_element_type=jnp.float32
    ).astype(jnp.bfloat16)
    attn_part = jnp.dot(
        heads_out.reshape(row_count, head_count * VDIM),
        out_proj,
        preferred_element_type=jnp.float32,
    )
    own_cols = lax.dynamic_slice_in_dim(attn_part, col_start, col_width, 1) + x_resid.astype(
        jnp.float32
    )
    resid_rows = lax.psum(
        lax.dynamic_update_slice_in_dim(attn_part, own_cols, col_start, 1).astype(jnp.bfloat16),
        "tp",
    ).astype(jnp.float32)
    resid_cols = lax.dynamic_slice_in_dim(resid_rows, col_start, col_width, 1)
    inv_rms = lax.rsqrt(jnp.mean(resid_rows * resid_rows, axis=1) + EPS)
    normed = resid_rows * inv_rms[:, None] * norm_gain.astype(jnp.float32)[None, :]
    logits = jnp.dot(normed, router.astype(jnp.float32).T, precision=lax.Precision.HIGHEST)
    outgoing = normed.astype(jnp.bfloat16)
    expert_ids = jnp.arange(expert_count, dtype=jnp.int32)
    onehot = routes[:, :, None] == expert_ids[None, None, :]
    chosen = jnp.sum(jnp.where(onehot, logits[:, None, :], 0.0), axis=2)
    gate_vals = jax.nn.sigmoid(chosen)
    gate_vals = ROUTE_SCALE * gate_vals / jnp.sum(gate_vals, axis=1, keepdims=True)
    hit_flags = onehot.astype(jnp.int32).reshape(row_count * TOP, expert_count)
    before = jnp.cumsum(hit_flags, axis=0) - hit_flags
    slot_ids = jnp.sum(before * hit_flags, axis=1)
    places = routes.reshape(row_count * TOP) * capacity + slot_ids
    send_width = outgoing.shape[1]
    buffer = (
        jnp.zeros((expert_count * capacity, send_width), jnp.bfloat16)
        .at[places]
        .set(jnp.repeat(outgoing, TOP, axis=0))
    )
    buffer = buffer.reshape(expert_count, capacity, send_width)
    arrived = lax.all_to_all(buffer, "ctx", split_axis=0, concat_axis=0, tiled=True)
    source_count, slot_count, full_width = arrived.shape
    slot_rows = arrived.reshape(source_count * slot_count, full_width)
    gate_part = jnp.dot(slot_rows, gate_proj[0], preferred_element_type=jnp.float32)
    up_part = jnp.dot(slot_rows, up_proj[0], preferred_element_type=jnp.float32)
    hidden = (jax.nn.silu(gate_part) * up_part).astype(jnp.bfloat16)
    down_part = jnp.dot(hidden, down_proj[0], preferred_element_type=jnp.float32).reshape(
        source_count, slot_count, full_width
    )
    summed = lax.psum_scatter(down_part.astype(jnp.bfloat16), "tp", scatter_dimension=2, tiled=True)
    returned = lax.all_to_all(summed, "ctx", split_axis=0, concat_axis=0, tiled=True)
    picked = returned.reshape(expert_count * capacity, col_width)[places].reshape(
        row_count, TOP, col_width
    )
    routed_sum = jnp.sum(gate_vals[:, :, None] * picked.astype(jnp.float32), axis=1)
    return (resid_cols + routed_sum).astype(jnp.bfloat16)


def solution(mesh):
    return jax.shard_map(
        body,
        mesh=mesh,
        in_specs=(
            P("ctx", "tp"),
            P("ctx", "tp"),
            P("ctx", "tp"),
            P(None, "ctx"),
            P(None, "ctx"),
            P("tp", None, None),
            P("tp", None, None),
            P("tp", None),
            P(),
            P(),
            P("ctx", None),
            P("ctx", None, "tp"),
            P("ctx", None, "tp"),
            P("ctx", "tp", None),
        ),
        out_specs=P("ctx", "tp"),
        check_vma=False,
    )
```

profile of v0, /device:TPU:0, one launch (start us, length us, event | category | flops | bytes accessed | tf_op | source)
XLA Modules:
  0.0 743.2 jit_solution(2783576149681246537)
XLA Ops:
  6.5 0.7 all-gather.2.cloned.1.call-update
  7.3 0.0 all-reduce.2.cloned.1.call-start
  7.3 1.1 copy.29
  8.4 28.2 %all_gather.7 = bf16[64,1024]{1,0:T(8,128)(2,1)S(1)} all-gather(bf16[64,128]{1,0:T(8,128)(2,1)} %param.18), channel_id=1, replica_groups=mesh['ctx'=8,'tp'=4] {'ctx'}, dimensions={1}, use_global_device_ids=true | all-gather | bytes 147456 | tf_op jit(solution)/shard_map/all_gather | solution.py:50
  36.7 0.1 iota_compare_fusion
  36.8 15.7 %all-gather.2.cloned.1.call-done = bf16[512,1024]{1,0:T(8,128)(2,1)} async-done(((bf16[512,128]{1,0:T(8,128)(2,1)}), bf16[512,1024]{1,0:T(8,128)(2,1)}) %all-gather.2.cloned.1.call-update) | async-done | bytes 1048592 | tf_op jit(solution)/shard_map/all_gather | solution.py:49
  52.5 7.6 %fusion.17 = f32[128,16,1024]{2,0,1:T(8,128)} fusion(bf16[16,128,512]{2,1,0:T(8,128)(2,1)S(1)} %copy-done, bf16[512,1024]{1,0:T(8,128)(2,1)} %all-gather.2.cloned.1.call-done, bf16[128,2048]{1,0:T(8,128)(2,1)} %param.15), kind=kOutput, calls=%fused_computation.26 | convolution fusion | flops 2416967680 | bytes 12058624 | tf_op jit(solution)/shard_map/thl,ls->ths/dot_general | solution.py:51
  60.1 5.3 select_reduce_fusion
  65.4 3.2 copy-done.2
  68.6 2.0 fusion.2
  70.7 7.5 %fusion.35 = bf16[16,128,128]{1,2,0:T(8,128)(2,1)S(1)} fusion(bf16[16,512,128]{2,1,0:T(8,128)(2,1)} %param.20, f32[128,16]{0,1:T(8,128)S(1)} %fusion.2, f32[128,16,1024]{2,0,1:T(8,128)} %copy-done.2, f32[128,16]{0,1:T(8,128)S(1)} %broadcast_maximum_fusion, pred[128,1024]{1,0:T(8,128)(4,1)S(1)} %iota_compare_fusion, bf16[512,1024]{1,0:T(8,128)(2,1)S(1)} %copy-done.5), kind=kOutput, calls=%fused_computation.35 | convolution fusion | flops 2424569856 | bytes 12206080 | tf_op jit(solution)/shard_map/thl,hlv->thv/dot_general | solution.py:65
  78.1 0.0 copy-start.6
  78.1 11.5 %fusion.52 = f32[128,7168]{1,0:T(8,128)S(1)} fusion(bf16[128,2048]{0,1:T(8,128)(2,1)S(1)} %bitcast.69, bf16[2048,7168]{1,0:T(8,128)(2,1)} %param.21), kind=kOutput, calls=%fused_computation.63 | convolution fusion | flops 3758096384 | bytes 33554432 | tf_op jit(solution)/shard_map/dot_general | solution.py:68
  89.7 0.2 add_dynamic-update-slice_fusion
  89.9 0.0 copy-start.7
  89.9 0.0 copy-start.8
  89.9 1.5 convert_element_type.64
  91.4 0.0 all-reduce.2.cloned.1.call-update
  91.4 0.4 reduce-scatter.2.cloned.1.call-start
  91.8 0.1 copy.33
  91.9 0.1 eq.39
  92.0 0.1 eq.35
  92.1 0.1 copy.32
  92.2 0.1 mul.89
  92.4 1.1 reduce-window.6
  93.5 0.2 slice_reduce_fusion
  93.8 0.1 fusion.47
  93.9 43.7 %all-reduce.2.cloned.1.call-done = bf16[128,7168]{1,0:T(8,128)(2,1)} async-done(((bf16[128,7168]{1,0:T(8,128)(2,1)}), bf16[128,7168]{1,0:T(8,128)(2,1)}) %all-reduce.2.cloned.1.call-update) | async-done | bytes 1835024 | tf_op jit(solution)/shard_map/psum | solution.py:76
  137.5 1.9 multiply_reduce_fusion.1
  139.5 2.0 fusion.14
  141.5 5.4 broadcast_in_dim.60
  146.9 12.1 %reshape.148 = bf16[512,7168]{1,0:T(8,128)(2,1)} reshape(bf16[128,4,7168]{2,1,0:T(4,128)(2,1)} %broadcast_in_dim.60) | data formatting | bytes 14680064 | tf_op jit(solution)/shard_map/reshape | solution.py:98
  159.0 20.5 %scatter_custom_fusion = bf16[1024,7168]{1,0:T(8,128)(2,1)} fusion(s32[512]{0:T(512)S(1)} %bitcast.70, bf16[512,7168]{1,0:T(8,128)(2,1)} %reshape.148, bf16[]{:T(256)} %constant.45.clone.1), kind=kCustom, calls=%fused_computation.6 | custom fusion | bytes 14680576 | tf_op jit(solution)/shard_map/scatter | solution.py:98
  179.5 323.6 %all_to_all.10 = bf16[8,128,7168]{2,1,0:T(8,128)(2,1)S(1)} all-to-all(bf16[8,128,7168]{2,1,0:T(8,128)(2,1)} %bitcast.64), channel_id=1, replica_groups=mesh['ctx'=8,'tp'=4] {'ctx'}, dimensions={0} | all-to-all | bytes 29360128 | tf_op jit(solution)/shard_map/all_to_all | solution.py:101
  503.2 3.9 fusion.12
  507.1 4.0 fusion.32
  511.1 7.4 convolution_convert_fusion
  518.5 0.0 reduce-scatter.2.cloned.1.call-update
  518.6 111.4 %reduce-scatter.2.cloned.1.call-done = bf16[8,128,1792]{2,1,0:T(8,128)(2,1)} async-done(((bf16[8,128,7168]{2,1,0:T(8,128)(2,1)}), bf16[8,128,1792]{2,1,0:T(8,128)(2,1)}) %reduce-scatter.2.cloned.1.call-update) | async-done | bytes 3670032 | tf_op jit(solution)/shard_map/reduce_scatter | solution.py:110
  629.9 5.8 all-to-all-start.1
  635.7 2.1 fusion.15
  638.0 0.1 copy.31
  638.1 2.2 convert_element_type.65
  640.2 77.4 %all-to-all-done.1 = bf16[8,128,1792]{2,1,0:T(8,128)(2,1)} async-done(((bf16[8,128,1792]{2,1,0:T(8,128)(2,1)}), bf16[8,128,1792]{2,1,0:T(8,128)(2,1)}, u32[]{:S(2)}, u32[]{:S(2)}) %all-to-all-start.1) | async-done | bytes 3670048 | tf_op jit(solution)/shard_map/all_to_all | solution.py:111
  717.7 7.3 gather_fusion
  725.0 4.7 reshape.135
  729.7 4.7 multiply_reduce_fusion
  734.4 2.1 add_convert_fusion
  (34 shorter events, 0.2 us)
Async XLA Ops:
  6.5 46.0 %copy-start = (bf16[16,128,512]{2,1,0:T(8,128)(2,1)S(1)}, bf16[16,128,512]{2,1,0:T(8,128)(2,1)}, u32[]{:S(2)}) copy-start(bf16[16,128,512]{2,1,0:T(8,128)(2,1)} %param.19) | copy-start | bytes 6291460
  6.5 46.0 %all-gather.2.cloned.1.call-start = ((), (), s32[]{:S(2)}) async-start(), calls=%async_computation.3 | async-start | bytes 1179648 | tf_op jit(solution)/shard_map/all_gather | solution.py:49
  7.3 130.3 %all-reduce.2.cloned.1.call-start = ((), (), s32[]{:S(2)}) async-start(), calls=%async_computation.4 | async-start | bytes 3670016 | tf_op jit(solution)/shard_map/psum | solution.py:76
  65.4 3.2 copy-start.2
  68.6 2.1 copy-start.5
  78.1 11.5 %copy-start.6 = (bf16[128,1792]{1,0:T(8,128)(2,1)S(1)}, bf16[128,1792]{1,0:T(8,128)(2,1)}, u32[]{:S(2)}) copy-start(bf16[128,1792]{1,0:T(8,128)(2,1)} %param.14) | copy-start | bytes 1376260
  89.9 1.9 copy-start.7
  89.9 3.9 copy-start.8
  91.4 538.5 %reduce-scatter.2.cloned.1.call-start = ((), (), s32[]{:S(2)}) async-start(), calls=%async_computation.5 | async-start | bytes 18350080 | tf_op jit(solution)/shard_map/reduce_scatter | solution.py:110
  179.5 323.6 %copy-start.9 = (bf16[1,7168,256]{2,1,0:T(8,128)(2,1)S(1)}, bf16[1,7168,256]{2,1,0:T(8,128)(2,1)}, u32[]{:S(2)}) copy-start(bf16[1,7168,256]{2,1,0:T(8,128)(2,1)} %param.25) | copy-start | bytes 11010052
  503.2 4.0 copy-start.10
  507.1 4.0 copy-start.4
  518.5 117.2 %copy-start.3 = (bf16[128,7168]{1,0:T(8,128)(2,1)S(1)}, bf16[128,7168]{1,0:T(8,128)(2,1)}, u32[]{:S(2)}) copy-start(bf16[128,7168]{1,0:T(8,128)(2,1)} %all-reduce.2.cloned.1.call-done) | copy-start | bytes 5505028
  518.6 117.2 %copy-start.11 = (bf16[8,7168]{1,0:T(8,128)(2,1)S(1)}, bf16[8,7168]{1,0:T(8,128)(2,1)}, u32[]{:S(2)}) copy-start(bf16[8,7168]{1,0:T(8,128)(2,1)} %param.23) | copy-start | bytes 344068
  629.9 87.8 %all-to-all-start.1 = ((bf16[8,128,1792]{2,1,0:T(8,128)(2,1)}), bf16[8,128,1792]{2,1,0:T(8,128)(2,1)}, u32[]{:S(2)}, u32[]{:S(2)}) async-start(bf16[8,128,1792]{2,1,0:T(8,128)(2,1)} %reduce-scatter.2.cloned.1.call-done), calls=%async_computation.2 | async-start | bytes 7340032 | tf_op jit(solution)/shard_map/all_to_all | solution.py:111
  725.0 11.4 %copy-start.1 = (bf16[16,128,512]{2,1,0:T(8,128)(2,1)S(1)}, bf16[16,128,512]{2,1,0:T(8,128)(2,1)}, u32[]{:S(2)}) copy-start(bf16[16,128,512]{2,1,0:T(8,128)(2,1)} %param.19) | copy-start | bytes 6291460
Sparse Core Ops, SparseCore 0:
  9.4 43.0 all-gather.1
  91.5 45.9 all-reduce.1
  518.7 111.2 reduce-scatter.1
where the time goes:
time: 752 us; the launch traced here: 743 us
  blocking collectives  352 us (47%)
  waiting for transfers between devices  249 us (33%)
  local copies, waits for them, and re-layouts  55.3 us (7%)
  matrix products  49.3 us (7%)
  other arithmetic  18.1 us (2%)
  between operations  13.6 us (2%)
    all_to_all x1, blocking collectives, body(): lax.all_to_all(buffer, 'ctx', split_axis=0, concat_axis=0, tiled=True)  324 us
    reduce_scatter x1, waiting for transfers between devices, body(): lax.psum_scatter(down_part.astype(jnp.bfloat16), 'tp', scatter_dimension=...  111 us
    all_to_all x1, waiting for transfers between devices, body(): lax.all_to_all(summed, 'ctx', split_axis=0, concat_axis=0, tiled=True)  77.4 us
    psum x1, waiting for transfers between devices, body(): lax.psum(lax.dynamic_update_slice_in_dim(attn_part, own_cols, col_start,...  43.7 us
    all_gather x1, blocking collectives, body(): rotary = lax.all_gather(key_rope, 'ctx', axis=1, tiled=True)  28.2 us
    scatter x1, local copies, waits for them, and re-layouts, body(): buffer = jnp.zeros((expert_count * capacity, send_width), jnp.bfloat16).a...  20.5 us
    all_gather x1, waiting for transfers between devices, body(): latent = lax.all_gather(latent_kv, 'ctx', axis=1, tiled=True)  15.7 us
  transfers between devices with their start and end apart: 4, of which 4 were waited for; matrix products, arithmetic and copies ran while one was open for 1% of the time, Pallas kernels for 0%

commit v1 on v0

v1 whole, which is shorter than its diff:
```python
import jax
import jax.numpy as jnp
from jax import lax
from jax.sharding import PartitionSpec as P

NOPE = 128
ROPE = 64
VDIM = 128
TOP = 4
CORES = 2
DEPTH = 4


EPS = 1e-06
ROUTE_SCALE = 2.5
LOW_SCORE = -1e30


def move(value, axis, outer, inner, d_outer, d_inner):
    pairs = []
    for o in range(outer):
        for i in range(inner):
            target = (o + d_outer) % outer * inner + (i + d_inner) % inner
            pairs.append((o * inner + i, target))
    return lax.ppermute(value, axis, pairs)


def body(
    x_resid,
    query_nope,
    query_rope,
    latent_kv,
    key_rope,
    absorb_key,
    absorb_value,
    out_proj,
    norm_gain,
    router,
    routes,
    gate_proj,
    up_proj,
    down_proj,
):
    row_count = x_resid.shape[0]
    col_width = x_resid.shape[1]
    head_count = absorb_key.shape[0]
    hid = gate_proj.shape[2]
    n_ctx = lax.axis_size("ctx")
    n_tp = lax.axis_size("tp")
    expert_count = n_ctx
    nz = DEPTH if n_ctx % DEPTH == 0 else 1
    nx = n_ctx // nz
    nc = CORES if n_tp % CORES == 0 else 1
    ny = n_tp // nc
    model_width = col_width * n_tp
    ctx = lax.axis_index("ctx")
    tp = lax.axis_index("tp")
    my_z, my_x = ctx // nx, ctx % nx
    my_y, my_c = tp // nc, tp % nc
    col_start = tp * col_width

    def over_ctx(value, dz, dx):
        return move(value, "ctx", nz, nx, dz, dx)

    def over_tp(value, dy, dc):
        return move(value, "tp", ny, nc, dy, dc)

    def tp_at(dy, dc):
        return (my_y + dy) % ny * nc + (my_c + dc) % nc

    def gather_ctx(value):
        column = [value]
        for _ in range(nz - 1):
            column.append(over_ctx(column[-1], 1, 0))
        return [[b] + [over_ctx(b, 0, dx) for dx in range(1, nx)] for b in column]

    keys = jnp.concatenate([latent_kv, key_rope], axis=0)
    key_blocks = gather_ctx(keys)

    gate_up = {}
    down = {}
    for dy in range(ny):
        for dc in range(nc):
            begin = tp_at(dy, dc) * col_width
            piece = jnp.concatenate(
                [
                    lax.dynamic_slice_in_dim(gate_proj[0], begin, col_width, 0),
                    lax.dynamic_slice_in_dim(up_proj[0], begin, col_width, 0),
                ],
                axis=1,
            )
            gate_up[dy, dc] = over_tp(piece, dy, dc) if (dy or dc) else piece
    for dy in range(ny):
        for dc in range(nc):
            begin = tp_at(dy, dc) * col_width
            piece = lax.dynamic_slice_in_dim(down_proj[0], begin, col_width, 1)
            down[dy, dc] = over_tp(piece, dy, dc) if (dy or dc) else piece

    query_pos = ctx * row_count + jnp.arange(row_count, dtype=jnp.int32)
    query_lat = jnp.einsum(
        "thn,hnl->thl",
        query_nope.reshape(row_count, head_count, NOPE),
        absorb_key,
        preferred_element_type=jnp.float32,
    ).astype(jnp.bfloat16)
    query_rot = query_rope.reshape(row_count, head_count, ROPE)
    score_scale = (NOPE + ROPE) ** (-0.5)
    all_keys = jnp.concatenate([b for line in key_blocks for b in line], axis=1)
    latent, rotary = all_keys[: latent_kv.shape[0]], all_keys[latent_kv.shape[0] :]
    owners = jnp.stack(
        [(my_z - dz) % nz * nx + (my_x - dx) % nx for dz in range(nz) for dx in range(nx)]
    )
    key_pos = (
        owners[:, None].astype(jnp.int32) * row_count
        + jnp.arange(row_count, dtype=jnp.int32)[None, :]
    ).reshape(n_ctx * row_count)
    scores = jnp.einsum("thl,ls->ths", query_lat, latent, preferred_element_type=jnp.float32)
    scores = (
        scores + jnp.einsum("thr,rs->ths", query_rot, rotary, preferred_element_type=jnp.float32)
    ) * score_scale
    allowed = (key_pos[None, :] <= query_pos[:, None])[:, None, :]
    top_score = jnp.max(jnp.where(allowed, scores, LOW_SCORE), axis=2)
    exp_scores = jnp.where(allowed, jnp.exp(scores - top_score[:, :, None]), 0.0)
    norm_sum = jnp.sum(exp_scores, axis=2)
    weighted = jnp.einsum(
        "ths,ls->thl", exp_scores.astype(jnp.bfloat16), latent, preferred_element_type=jnp.float32
    )
    attn_lat = (weighted / norm_sum[:, :, None]).astype(jnp.bfloat16)
    heads_out = jnp.einsum(
        "thl,hlv->thv", attn_lat, absorb_value, preferred_element_type=jnp.float32
    ).astype(jnp.bfloat16)
    attn_part = jnp.dot(
        heads_out.reshape(row_count, head_count * VDIM),
        out_proj,
        preferred_element_type=jnp.float32,
    )

    def own_part(dy, dc):
        return lax.dynamic_slice_in_dim(attn_part, tp_at(dy, dc) * col_width, col_width, 1)

    held = {dy: own_part(dy, 0) for dy in range(ny)}
    for dc in range(1, nc):
        for dy in range(ny):
            held[dy] = held[dy] + over_tp(own_part(dy, dc).astype(jnp.bfloat16), 0, dc).astype(
                jnp.float32
            )
    residual = x_resid.astype(jnp.float32) + held[0]
    for dy in range(1, ny):
        residual = residual + over_tp(held[dy].astype(jnp.bfloat16), dy, 0).astype(jnp.float32)

    gain = lax.dynamic_slice_in_dim(norm_gain, col_start, col_width, 0).astype(jnp.float32)
    scaled = residual * gain[None, :]
    token_blocks = gather_ctx(scaled.astype(jnp.bfloat16))

    router_cols = lax.dynamic_slice_in_dim(router, col_start, col_width, 1).astype(jnp.float32)
    stats = jnp.concatenate(
        [
            lax.dot_general(
                router_cols, scaled, (((1,), (1,)), ((), ())), precision=lax.Precision.HIGHEST
            ),
            jnp.sum(residual * residual, axis=1)[None, :],
        ],
        axis=0,
    )
    for dc in range(1, nc):
        stats = stats + over_tp(stats, 0, dc) if nc == 2 else stats
    stats = sum([over_tp(stats, dy, 0) for dy in range(1, ny)], stats)
    inv_rms = lax.rsqrt(stats[expert_count] / model_width + EPS)
    logits = stats[:expert_count] * inv_rms[None, :]
    expert_ids = jnp.arange(expert_count, dtype=jnp.int32)
    onehot = routes.T[:, None, :] == expert_ids[None, :, None]
    chosen = jnp.sum(jnp.where(onehot, logits[None, :, :], 0.0), axis=1)
    gate_vals = jax.nn.sigmoid(chosen)
    gate_vals = ROUTE_SCALE * gate_vals / jnp.sum(gate_vals, axis=0, keepdims=True)
    dense_gates = jnp.sum(jnp.where(onehot, gate_vals[:, None, :], 0.0), axis=0)
    meta_blocks = gather_ctx(jnp.concatenate([dense_gates, inv_rms[None, :]], axis=0))

    down_mat = jnp.concatenate(
        [down[dy, dc] for dc in range(nc) for dy in range(ny)], axis=0
    )

    def experts(dz):
        rows = jnp.concatenate(token_blocks[dz], axis=0)
        meta = jnp.concatenate(meta_blocks[dz], axis=1)
        row_scale = meta[expert_count][:, None]
        row_gate = lax.dynamic_slice_in_dim(meta, ctx, 1, 0)[0][:, None]

        def product(dy, dc):
            return jnp.dot(rows, gate_up[dy, dc], preferred_element_type=jnp.float32)

        sums = [None] * ny
        for dc in list(range(1, nc)):
            away = jnp.concatenate(
                [product(dy, dc).astype(jnp.bfloat16) for dy in range(ny)], axis=1
            )
            away = over_tp(away, 0, -dc).astype(jnp.float32)
            for dy in range(ny):
                term = away[:, dy * 2 * hid : (dy + 1) * 2 * hid]
                sums[dy] = term if sums[dy] is None else sums[dy] + term
        for dy in range(ny):
            mine = product(dy, 0)
            sums[dy] = mine if sums[dy] is None else sums[dy] + mine
        total = sums[0]
        for dy in range(1, ny):
            total = total + over_tp(sums[dy].astype(jnp.bfloat16), -dy, 0).astype(jnp.float32)
        total = total * row_scale
        hidden = (jax.nn.silu(total[:, :hid]) * total[:, hid:]).astype(jnp.bfloat16)
        line = jnp.concatenate(
            [hidden] + [over_tp(hidden, dy, 0) for dy in range(1, ny)], axis=1
        )
        whole = jnp.concatenate([line] + [over_tp(line, 0, dc) for dc in range(1, nc)], axis=1)
        out = jnp.dot(whole, down_mat, preferred_element_type=jnp.float32) * row_gate
        acc = out[:row_count]
        for dx in range(1, nx):
            other = out[dx * row_count : (dx + 1) * row_count].astype(jnp.bfloat16)
            acc = acc + over_ctx(other, 0, -dx).astype(jnp.float32)
        return acc

    parts = [experts(dz) for dz in range(nz)]
    total = None
    for dz in list(range(1, nz)):
        total = parts[dz] if total is None else total + parts[dz]
        total = over_ctx(total.astype(jnp.bfloat16), 1, 0).astype(jnp.float32)
    routed_sum = parts[0] if total is None else total + parts[0]
    return (residual + routed_sum).astype(jnp.bfloat16)


def solution(mesh):
    return jax.shard_map(
        body,
        mesh=mesh,
        in_specs=(
            P("ctx", "tp"),
            P("ctx", "tp"),
            P("ctx", "tp"),
            P(None, "ctx"),
            P(None, "ctx"),
            P("tp", None, None),
            P("tp", None, None),
            P("tp", None),
            P(),
            P(),
            P("ctx", None),
            P("ctx", None, "tp"),
            P("ctx", None, "tp"),
            P("ctx", "tp", None),
        ),
        out_specs=P("ctx", "tp"),
        check_vma=False,
    )
```

time: 752 us -> 358 us (0.48); the launches traced: 743 us -> 358 us
  blocking collectives: 352 us -> 0 us
  local copies, waits for them, and re-layouts: 55.3 us -> 16.6 us
  starting transfers between devices: 6.18 us -> 40.1 us
  waiting for transfers between devices: 249 us -> 222 us
  matrix products: 49.3 us -> 64.5 us
  between operations: 13.6 us -> 0.87 us
    all_to_all x1 -> x0, blocking collectives: 324 us -> none  [body(): lax.all_to_all(buffer, 'ctx', split_axis=0, concat_axis=0, tiled=True)]
    ppermute x0 -> x55, waiting for transfers between devices: none -> 222 us  [move(): return lax.ppermute(value, axis, pairs)]
    reduce_scatter x1 -> x0, waiting for transfers between devices: 111 us -> none  [body(): lax.psum_scatter(down_part.astype(jnp.bfloat16), 'tp', scatter_dimension=...]
    all_to_all x1 -> x0, waiting for transfers between devices: 77.4 us -> none  [body(): lax.all_to_all(summed, 'ctx', split_axis=0, concat_axis=0, tiled=True)]
    psum x1 -> x0, waiting for transfers between devices: 43.7 us -> none  [body(): lax.psum(lax.dynamic_update_slice_in_dim(attn_part, own_cols, col_start,...]
    ppermute x0 -> x55, starting transfers between devices: none -> 40.1 us  [move(): return lax.ppermute(value, axis, pairs)]
    all_gather x1 -> x0, blocking collectives: 28.2 us -> none  [body(): rotary = lax.all_gather(key_rope, 'ctx', axis=1, tiled=True)]
    scatter x1 -> x0, local copies, waits for them, and re-layouts: 20.5 us -> none  [body(): buffer = jnp.zeros((expert_count * capacity, send_width), jnp.bfloat16).a...]
  transfers between devices with their start and end apart: 4 -> 55, of which waited for: 4 -> 32; matrix products, arithmetic and copies ran while one was open for 1% -> 14% of each run, Pallas kernels for 0% -> 0%
where the time goes in v1:
time: 358 us
  waiting for transfers between devices  222 us (62%)
  matrix products  64.5 us (18%)
  starting transfers between devices  40.1 us (11%)
  local copies, waits for them, and re-layouts  16.6 us (5%)
  other arithmetic  13 us (4%)
    ppermute x55, waiting for transfers between devices, move(): return lax.ppermute(value, axis, pairs)  222 us
    ppermute x55, starting transfers between devices, move(): return lax.ppermute(value, axis, pairs)  40.1 us
    dot_general x16, matrix products, product(): return jnp.dot(rows, gate_up[dy, dc], preferred_element_type=jnp.float32)  22.3 us
    sub x1, matrix products, body(): scores - top_score[:, :, None]  11.7 us
    dot_general x1, matrix products, body(): jnp.dot(heads_out.reshape(row_count, head_count * VDIM), out_proj, prefer...  11.5 us
    unnamed x42, local copies, waits for them, and re-layouts  7.67 us
    dot_general x1, matrix products, body(): jnp.einsum('thl,ls->ths', query_lat, latent, preferred_element_type=jnp.f...  7.29 us
  transfers between devices with their start and end apart: 55, of which 32 were waited for; matrix products, arithmetic and copies ran while one was open for 14% of the time, Pallas kernels for 0%

profile of v1, /device:TPU:0, one launch (start us, length us, event | category | flops | bytes accessed | tf_op | source)
XLA Modules:
  0.0 357.5 jit_solution(8178189425386393019)
XLA Ops:
  0.0 1.7 constant_dynamic-update-slice_fusion.1
  3.1 2.9 collective-permute-start
  9.7 3.8 %collective-permute-done.1 = bf16[576,128]{1,0:T(8,128)(2,1)} collective-permute-done((bf16[576,128]{1,0:T(8,128)(2,1)}, bf16[576,128]{1,0:T(8,128)(2,1)}, u32[]{:S(2)}, u32[]{:S(2)}) %collective-permute-start.1) | collective-permute-done | bytes 147488 | tf_op jit(solution)/shard_map/ppermute | solution.py:25
  16.0 5.2 %collective-permute-done.3 = bf16[576,128]{1,0:T(8,128)(2,1)S(1)} collective-permute-done((bf16[576,128]{1,0:T(8,128)(2,1)}, bf16[576,128]{1,0:T(8,128)(2,1)S(1)}, u32[]{:S(2)}, u32[]{:S(2)}) %collective-permute-start.3) | collective-permute-done | bytes 147488 | tf_op jit(solution)/shard_map/ppermute | solution.py:25
  22.8 6.8 %collective-permute-done.5 = bf16[576,128]{1,0:T(8,128)(2,1)S(1)} collective-permute-done((bf16[576,128]{1,0:T(8,128)(2,1)S(1)}, bf16[576,128]{1,0:T(8,128)(2,1)S(1)}, u32[]{:S(2)}, u32[]{:S(2)}) %collective-permute-start.5) | collective-permute-done | bytes 147488 | tf_op jit(solution)/shard_map/ppermute | solution.py:25
  30.3 4.5 %collective-permute-done.6 = bf16[576,128]{1,0:T(8,128)(2,1)S(1)} collective-permute-done((bf16[576,128]{1,0:T(8,128)(2,1)S(1)}, bf16[576,128]{1,0:T(8,128)(2,1)S(1)}, u32[]{:S(2)}, u32[]{:S(2)}) %collective-permute-start.6) | collective-permute-done | bytes 147488 | tf_op jit(solution)/shard_map/ppermute | solution.py:25
  34.9 7.3 %fusion.10 = f32[128,16,1024]{2,0,1:T(8,128)} fusion(bf16[16,128,512]{2,1,0:T(8,128)(2,1)S(1)} %copy-done, bf16[576,1024]{1,0:T(8,128)(2,1)S(1)} %constant_dynamic-update-slice_fusion.2, bf16[128,2048]{1,0:T(8,128)(2,1)} %param.15), kind=kOutput, calls=%fused_computation.13 | convolution fusion | flops 2416967680 | bytes 12058624 | tf_op jit(solution)/shard_map/thl,ls->ths/dot_general | solution.py:117
  42.2 11.7 %fusion.104 = (f32[128,16]{0,1:T(8,128)S(1)}, bf16[128,16,1024]{2,0,1:T(8,128)(2,1)}) fusion(pred[128,1024]{1,0:T(8,128)(4,1)} %broadcast_compare_fusion, f32[128,16,1024]{2,0,1:T(8,128)} %fusion.10, bf16[128,16,64]{0,2,1:T(8,128)(2,1)S(1)} %bitcast.125, bf16[576,1024]{1,0:T(8,128)(2,1)S(1)} %constant_dynamic-update-slice_fusion.2), kind=kOutput, calls=%fused_computation.197 | convolution fusion | flops 555746304 | bytes 22028288 | tf_op jit(solution)/shard_map/sub | solution.py:123
  53.8 5.9 %fusion.20 = bf16[16,128,128]{1,2,0:T(8,128)(2,1)S(1)} fusion(bf16[16,512,128]{2,1,0:T(8,128)(2,1)} %param.20, f32[128,16]{0,1:T(8,128)S(1)} %get-tuple-element.33, bf16[128,16,1024]{2,0,1:T(8,128)(2,1)} %get-tuple-element.34, bf16[576,1024]{1,0:T(8,128)(2,1)S(1)} %constant_dynamic-update-slice_fusion.2), kind=kOutput, calls=%fused_computation.22 | convolution fusion | flops 2418278400 | bytes 7872512 | tf_op jit(solution)/shard_map/thl,hlv->thv/dot_general | solution.py:129
  59.8 11.5 %fusion.105 = f32[128,7168]{1,0:T(8,128)S(1)} fusion(bf16[128,2048]{0,1:T(8,128)(2,1)S(1)} %bitcast.124, bf16[2048,7168]{1,0:T(8,128)(2,1)} %param.21), kind=kOutput, calls=%fused_computation.198 | convolution fusion | flops 3758096384 | bytes 33554432 | tf_op jit(solution)/shard_map/dot_general | solution.py:132
  71.3 1.8 copy-done.2
  75.0 2.0 add_convert_fusion
  78.6 5.1 %dynamic-slice_bitcast_fusion.6 = (bf16[1792,256]{1,0:T(8,128)(2,1)}, bf16[1792,256]{1,0:T(8,128)(2,1)}, bf16[1792,256]{1,0:T(8,128)(2,1)S(1)}, bf16[1792,256]{1...) fusion(bf16[1,7168,256]{2,1,0:T(8,128)(2,1)} %param.26, ...), kind=kLoop, calls=%fused_computation.69 | loop fusion | bytes 14680080 | tf_op jit(solution)/shard_map/dynamic_slice | solution.py:88
  86.7 3.3 collective-permute-done.9
  89.9 2.5 multiply_convert_fusion
  95.4 1.6 collective-permute-start.13
  97.6 1.9 dynamic-slice_bitcast_fusion.3
  99.5 38.6 %collective-permute-done.18 = f32[9,128]{1,0:T(8,128)S(1)} collective-permute-done((f32[9,128]{1,0:T(8,128)S(1)}, f32[9,128]{1,0:T(8,128)S(1)}, u32[]{:S(2)}, u32[]{:S(2)}) %collective-permute-start.18) | collective-permute-done | bytes 4640 | tf_op jit(solution)/shard_map/ppermute | solution.py:25
  140.4 3.4 collective-permute-done.19
  144.3 9.6 %collective-permute-done.32 = f32[9,128]{1,0:T(8,128)S(1)} collective-permute-done((f32[9,128]{1,0:T(8,128)S(1)}, f32[9,128]{1,0:T(8,128)S(1)}, u32[]{:S(2)}, u32[]{:S(2)}) %collective-permute-start.32) | collective-permute-done | bytes 4640 | tf_op jit(solution)/shard_map/ppermute | solution.py:25
  155.4 2.2 collective-permute-done.20
  159.1 2.2 collective-permute-done.33
  161.3 5.4 %collective-permute-done.42 = f32[9,128]{1,0:T(8,128)S(1)} collective-permute-done((f32[9,128]{1,0:T(8,128)S(1)}, f32[9,128]{1,0:T(8,128)S(1)}, u32[]{:S(2)}, u32[]{:S(2)}) %collective-permute-start.42) | collective-permute-done | bytes 4640 | tf_op jit(solution)/shard_map/ppermute | solution.py:25
  168.2 2.2 collective-permute-done.43
  174.0 2.1 convolution_convert_fusion.1
  176.2 2.1 convolution_convert_fusion
  178.6 6.8 %collective-permute-done.11 = bf16[128,1792]{1,0:T(8,128)(2,1)S(1)} collective-permute-done((bf16[128,1792]{1,0:T(8,128)(2,1)S(1)}, bf16[128,1792]{1,0:T(8,128)(2,1)S(1)}, u32[]{:S(2)}, u32[]{:S(2)}) %collective-permute-start.11) | collective-permute-done | bytes 458784 | tf_op jit(solution)/shard_map/ppermute | solution.py:25
  185.4 2.1 convolution_convert_fusion.7
  187.6 2.2 convolution_convert_fusion.6
  190.8 22.7 %collective-permute-done.15 = bf16[1792,512]{1,0:T(8,128)(2,1)S(1)} collective-permute-done((bf16[1792,512]{1,0:T(8,128)(2,1)}, bf16[1792,512]{1,0:T(8,128)(2,1)S(1)}, u32[]{:S(2)}, u32[]{:S(2)}) %collective-permute-start.15) | collective-permute-done | bytes 1835040 | tf_op jit(solution)/shard_map/ppermute | solution.py:25
  215.9 35.1 %collective-permute-done.50 = bf16[256,512]{1,0:T(8,128)(2,1)S(1)} collective-permute-done((bf16[256,512]{1,0:T(8,128)(2,1)S(1)}, bf16[256,512]{1,0:T(8,128)(2,1)S(1)}, u32[]{:S(2)}, u32[]{:S(2)}) %collective-permute-start.50) | collective-permute-done | bytes 262176 | tf_op jit(solution)/shard_map/ppermute | solution.py:25
  253.3 6.2 %collective-permute-done.29 = bf16[128,1792]{1,0:T(8,128)(2,1)S(1)} collective-permute-done((bf16[128,1792]{1,0:T(8,128)(2,1)S(1)}, bf16[128,1792]{1,0:T(8,128)(2,1)S(1)}, u32[]{:S(2)}, u32[]{:S(2)}) %collective-permute-start.29) | collective-permute-done | bytes 458784 | tf_op jit(solution)/shard_map/ppermute | solution.py:25
  259.6 2.1 convolution_convert_fusion.5
  261.7 2.1 convolution_convert_fusion.4
  266.3 2.7 collective-permute-done.52
  270.6 4.7 %collective-permute-done.16 = bf16[256,512]{1,0:T(8,128)(2,1)S(1)} collective-permute-done((bf16[256,512]{1,0:T(8,128)(2,1)S(1)}, bf16[256,512]{1,0:T(8,128)(2,1)S(1)}, u32[]{:S(2)}, u32[]{:S(2)}) %collective-permute-start.16) | collective-permute-done | bytes 262176 | tf_op jit(solution)/shard_map/ppermute | solution.py:25
  277.6 6.3 %collective-permute-done.39 = bf16[128,1792]{1,0:T(8,128)(2,1)S(1)} collective-permute-done((bf16[128,1792]{1,0:T(8,128)(2,1)S(1)}, bf16[128,1792]{1,0:T(8,128)(2,1)S(1)}, u32[]{:S(2)}, u32[]{:S(2)}) %collective-permute-start.39) | collective-permute-done | bytes 458784 | tf_op jit(solution)/shard_map/ppermute | solution.py:25
  285.4 2.1 convolution_convert_fusion.3
  288.8 2.1 convolution_convert_fusion.2
  291.2 3.5 collective-permute-done.31
  304.0 5.0 %collective-permute-done.41 = bf16[256,512]{1,0:T(8,128)(2,1)S(1)} collective-permute-done((bf16[256,512]{1,0:T(8,128)(2,1)S(1)}, bf16[256,512]{1,0:T(8,128)(2,1)S(1)}, u32[]{:S(2)}, u32[]{:S(2)}) %collective-permute-start.41) | collective-permute-done | bytes 262176 | tf_op jit(solution)/shard_map/ppermute | solution.py:25
  310.3 2.8 collective-permute-done.26
  319.4 7.3 %collective-permute-done.27 = bf16[128,1792]{1,0:T(8,128)(2,1)S(1)} collective-permute-done((bf16[128,1792]{1,0:T(8,128)(2,1)S(1)}, bf16[128,1792]{1,0:T(8,128)(2,1)S(1)}, u32[]{:S(2)}, u32[]{:S(2)}) %collective-permute-start.27) | collective-permute-done | bytes 458784 | tf_op jit(solution)/shard_map/ppermute | solution.py:25
  326.7 2.7 collective-permute-done.36
  332.4 6.9 %collective-permute-done.46 = bf16[128,1792]{1,0:T(8,128)(2,1)S(1)} collective-permute-done((bf16[128,1792]{1,0:T(8,128)(2,1)S(1)}, bf16[128,1792]{1,0:T(8,128)(2,1)S(1)}, u32[]{:S(2)}, u32[]{:S(2)}) %collective-permute-start.46) | collective-permute-done | bytes 458784 | tf_op jit(solution)/shard_map/ppermute | solution.py:25
  339.3 4.2 %collective-permute-done.37 = bf16[128,1792]{1,0:T(8,128)(2,1)S(1)} collective-permute-done((bf16[128,1792]{1,0:T(8,128)(2,1)S(1)}, bf16[128,1792]{1,0:T(8,128)(2,1)S(1)}, u32[]{:S(2)}, u32[]{:S(2)}) %collective-permute-start.37) | collective-permute-done | bytes 458784 | tf_op jit(solution)/shard_map/ppermute | solution.py:25
  343.6 5.0 %collective-permute-done.54 = bf16[128,1792]{1,0:T(8,128)(2,1)S(1)} collective-permute-done((bf16[128,1792]{1,0:T(8,128)(2,1)S(1)}, bf16[128,1792]{1,0:T(8,128)(2,1)S(1)}, u32[]{:S(2)}, u32[]{:S(2)}) %collective-permute-start.54) | collective-permute-done | bytes 458784 | tf_op jit(solution)/shard_map/ppermute | solution.py:25
  348.7 7.8 %collective-permute-done.47 = bf16[128,1792]{1,0:T(8,128)(2,1)S(1)} collective-permute-done((bf16[128,1792]{1,0:T(8,128)(2,1)S(1)}, bf16[128,1792]{1,0:T(8,128)(2,1)S(1)}, u32[]{:S(2)}, u32[]{:S(2)}) %collective-permute-start.47) | collective-permute-done | bytes 458784 | tf_op jit(solution)/shard_map/ppermute | solution.py:25
  (191 shorter events, 66.6 us)
Async XLA Ops:
  3.1 11.0 %collective-permute-start = (bf16[576,128]{1,0:T(8,128)(2,1)}, bf16[576,128]{1,0:T(8,128)(2,1)}, u32[]{:S(2)}, u32[]{:S(2)}) collective-permute-start(bf16[576,128]{1,0:T(8,128)(2,1)} %get-tuple-element.31), channel_id=1, source_target_pairs={{0,4},{4,0},{8,12},{12,8},{16,20},{20,16},{24,28},{28,24},{1,5},{5... | collective-permute-start | bytes 442376 | tf_op jit(solution)/shard_map/ppermute | solution.py:25
  6.0 7.5 %collective-permute-start.1 = (bf16[576,128]{1,0:T(8,128)(2,1)}, bf16[576,128]{1,0:T(8,128)(2,1)}, u32[]{:S(2)}, u32[]{:S(2)}) collective-permute-start(bf16[576,128]{1,0:T(8,128)(2,1)} %get-tuple-element.31), channel_id=1, source_target_pairs={{0,8},{4,12},{8,16},{12,20},{16,24},{20,28},{24,0},{28,4},{1,9},{5... | collective-permute-start | bytes 442376 | tf_op jit(solution)/shard_map/ppermute | solution.py:25
  13.5 9.2 %collective-permute-start.2 = (bf16[576,128]{1,0:T(8,128)(2,1)}, bf16[576,128]{1,0:T(8,128)(2,1)S(1)}, u32[]{:S(2)}, u32[]{:S(2)}) collective-permute-start(bf16[576,128]{1,0:T(8,128)(2,1)} %collective-permute-done.1), channel_id=1, source_target_pairs={{0,4},{4,0},{8,12},{12,8},{16,20},{20,16},{24,28},{28,24},{1,5},{5... | collective-permute-start | bytes 442376 | tf_op jit(solution)/shard_map/ppermute | solution.py:25
  14.1 7.2 %collective-permute-start.3 = (bf16[576,128]{1,0:T(8,128)(2,1)}, bf16[576,128]{1,0:T(8,128)(2,1)S(1)}, u32[]{:S(2)}, u32[]{:S(2)}) collective-permute-start(bf16[576,128]{1,0:T(8,128)(2,1)} %collective-permute-done.1), channel_id=1, source_target_pairs={{0,8},{4,12},{8,16},{12,20},{16,24},{20,28},{24,0},{28,4},{1,9},{5... | collective-permute-start | bytes 442376 | tf_op jit(solution)/shard_map/ppermute | solution.py:25
  21.2 9.0 %collective-permute-start.4 = (bf16[576,128]{1,0:T(8,128)(2,1)S(1)}, bf16[576,128]{1,0:T(8,128)(2,1)S(1)}, u32[]{:S(2)}, u32[]{:S(2)}) collective-permute-start(bf16[576,128]{1,0:T(8,128)(2,1)S(1)} %collective-permute-done.3), channel_id=1, source_target_pairs={{0,4},{4,0},{8,12},{12,8},{16,20},{20,16},{24,28},{28,24},{1,5},{5... | collective-permute-start | bytes 442376 | tf_op jit(solution)/shard_map/ppermute | solution.py:25
  22.7 6.9 %collective-permute-start.5 = (bf16[576,128]{1,0:T(8,128)(2,1)S(1)}, bf16[576,128]{1,0:T(8,128)(2,1)S(1)}, u32[]{:S(2)}, u32[]{:S(2)}) collective-permute-start(bf16[576,128]{1,0:T(8,128)(2,1)S(1)} %collective-permute-done.3), channel_id=1, source_target_pairs={{0,8},{4,12},{8,16},{12,20},{16,24},{20,28},{24,0},{28,4},{1,9},{5... | collective-permute-start | bytes 442376 | tf_op jit(solution)/shard_map/ppermute | solution.py:25
  29.7 5.1 %collective-permute-start.6 = (bf16[576,128]{1,0:T(8,128)(2,1)S(1)}, bf16[576,128]{1,0:T(8,128)(2,1)S(1)}, u32[]{:S(2)}, u32[]{:S(2)}) collective-permute-start(bf16[576,128]{1,0:T(8,128)(2,1)S(1)} %collective-permute-done.5), channel_id=1, source_target_pairs={{0,4},{4,0},{8,12},{12,8},{16,20},{20,16},{24,28},{28,24},{1,5},{5... | collective-permute-start | bytes 442376 | tf_op jit(solution)/shard_map/ppermute | solution.py:25
  73.3 12.6 %collective-permute-start.7 = (bf16[128,1792]{1,0:T(8,128)(2,1)S(1)}, bf16[128,1792]{1,0:T(8,128)(2,1)S(1)}, u32[]{:S(2)}, u32[]{:S(2)}) collective-permute-start(bf16[128,1792]{1,0:T(8,128)(2,1)S(1)} %get-tuple-element.19), channel_id=1, source_target_pairs={{0,1},{1,0},{2,3},{3,2},{4,5},{5,4},{6,7},{7,6},{8,9},{9,8},{10,11... | collective-permute-start | bytes 1376264 | tf_op jit(solution)/shard_map/ppermute | solution.py:25
  77.1 12.9 %collective-permute-start.9 = (bf16[128,1792]{1,0:T(8,128)(2,1)}, bf16[128,1792]{1,0:T(8,128)(2,1)}, u32[]{:S(2)}, u32[]{:S(2)}) collective-permute-start(bf16[128,1792]{1,0:T(8,128)(2,1)} %add_convert_fusion), channel_id=1, source_target_pairs={{0,2},{1,3},{2,0},{3,1},{4,6},{5,7},{6,4},{7,5},{8,10},{9,11},{10,... | collective-permute-start | bytes 1376264 | tf_op jit(solution)/shard_map/ppermute | solution.py:25
  85.1 86.8 %collective-permute-start.12 = (bf16[1792,512]{1,0:T(8,128)(2,1)}, bf16[1792,512]{1,0:T(8,128)(2,1)}, u32[]{:S(2)}, u32[]{:S(2)}) collective-permute-start(bf16[1792,512]{1,0:T(8,128)(2,1)} %pad_maximum_fusion.1), channel_id=1, source_target_pairs={{0,1},{1,0},{2,3},{3,2},{4,5},{5,4},{6,7},{7,6},{8,9},{9,8},{10,11... | collective-permute-start | bytes 5505032 | tf_op jit(solution)/shard_map/ppermute | solution.py:25
  95.4 80.7 %collective-permute-start.13 = (bf16[1792,512]{1,0:T(8,128)(2,1)}, bf16[1792,512]{1,0:T(8,128)(2,1)}, u32[]{:S(2)}, u32[]{:S(2)}) collective-permute-start(bf16[1792,512]{1,0:T(8,128)(2,1)} %pad_maximum_fusion.2), channel_id=1, source_target_pairs={{0,3},{1,2},{2,1},{3,0},{4,7},{5,6},{6,5},{7,4},{8,11},{9,10},{10,... | collective-permute-start | bytes 5505032 | tf_op jit(solution)/shard_map/ppermute | solution.py:25
  97.0 41.1 %collective-permute-start.18 = (f32[9,128]{1,0:T(8,128)S(1)}, f32[9,128]{1,0:T(8,128)S(1)}, u32[]{:S(2)}, u32[]{:S(2)}) collective-permute-start(f32[9,128]{1,0:T(8,128)S(1)} %fusion.90), channel_id=1, source_target_pairs={{0,2},{1,3},{2,0},{3,1},{4,6},{5,7},{6,4},{7,5},{8,10},{9,11},{10,... | collective-permute-start | bytes 13832 | tf_op jit(solution)/shard_map/ppermute | solution.py:25
  138.2 5.5 %collective-permute-start.19 = (f32[9,128]{1,0:T(8,128)S(1)}, f32[9,128]{1,0:T(8,128)S(1)}, u32[]{:S(2)}, u32[]{:S(2)}) collective-permute-start(f32[9,128]{1,0:T(8,128)S(1)} %pad_maximum_fusion.16), channel_id=1, source_target_pairs={{0,8},{4,12},{8,16},{12,20},{16,24},{20,28},{24,0},{28,4},{1,9},{5... | collective-permute-start | bytes 13832 | tf_op jit(solution)/shard_map/ppermute | solution.py:25
  138.3 6.0 %collective-permute-start.51 = (f32[9,128]{1,0:T(8,128)S(1)}, f32[9,128]{1,0:T(8,128)S(1)}, u32[]{:S(2)}, u32[]{:S(2)}) collective-permute-start(f32[9,128]{1,0:T(8,128)S(1)} %pad_maximum_fusion.16), channel_id=1, source_target_pairs={{0,4},{4,0},{8,12},{12,8},{16,20},{20,16},{24,28},{28,24},{1,5},{5... | collective-permute-start | bytes 13832 | tf_op jit(solution)/shard_map/ppermute | solution.py:25
  140.4 32.1 %collective-permute-start.10 = (bf16[128,1792]{1,0:T(8,128)(2,1)S(1)}, bf16[128,1792]{1,0:T(8,128)(2,1)S(1)}, u32[]{:S(2)}, u32[]{:S(2)}) collective-permute-start(bf16[128,1792]{1,0:T(8,128)(2,1)S(1)} %copy-done.11), channel_id=1, source_target_pairs={{0,8},{4,12},{8,16},{12,20},{16,24},{20,28},{24,0},{28,4},{1,9},{5... | collective-permute-start | bytes 1376264 | tf_op jit(solution)/shard_map/ppermute | solution.py:25
  143.7 28.7 %collective-permute-start.48 = (bf16[128,1792]{1,0:T(8,128)(2,1)S(1)}, bf16[128,1792]{1,0:T(8,128)(2,1)S(1)}, u32[]{:S(2)}, u32[]{:S(2)}) collective-permute-start(bf16[128,1792]{1,0:T(8,128)(2,1)S(1)} %copy-done.11), channel_id=1, source_target_pairs={{0,4},{4,0},{8,12},{12,8},{16,20},{20,16},{24,28},{28,24},{1,5},{5... | collective-permute-start | bytes 1376264 | tf_op jit(solution)/shard_map/ppermute | solution.py:25
  144.3 9.6 %collective-permute-start.32 = (f32[9,128]{1,0:T(8,128)S(1)}, f32[9,128]{1,0:T(8,128)S(1)}, u32[]{:S(2)}, u32[]{:S(2)}) collective-permute-start(f32[9,128]{1,0:T(8,128)S(1)} %collective-permute-done.19), channel_id=1, source_target_pairs={{0,8},{4,12},{8,16},{12,20},{16,24},{20,28},{24,0},{28,4},{1,9},{5... | collective-permute-start | bytes 13832 | tf_op jit(solution)/shard_map/ppermute | solution.py:25
  153.9 3.7 %collective-permute-start.20 = (f32[9,128]{1,0:T(8,128)S(1)}, f32[9,128]{1,0:T(8,128)S(1)}, u32[]{:S(2)}, u32[]{:S(2)}) collective-permute-start(f32[9,128]{1,0:T(8,128)S(1)} %collective-permute-done.19), channel_id=1, source_target_pairs={{0,4},{4,0},{8,12},{12,8},{16,20},{20,16},{24,28},{28,24},{1,5},{5... | collective-permute-start | bytes 13832 | tf_op jit(solution)/shard_map/ppermute | solution.py:25
  161.2 5.4 %collective-permute-start.42 = (f32[9,128]{1,0:T(8,128)S(1)}, f32[9,128]{1,0:T(8,128)S(1)}, u32[]{:S(2)}, u32[]{:S(2)}) collective-permute-start(f32[9,128]{1,0:T(8,128)S(1)} %collective-permute-done.32), channel_id=1, source_target_pairs={{0,8},{4,12},{8,16},{12,20},{16,24},{20,28},{24,0},{28,4},{1,9},{5... | collective-permute-start | bytes 13832 | tf_op jit(solution)/shard_map/ppermute | solution.py:25
  170.3 43.2 %collective-permute-start.15 = (bf16[1792,512]{1,0:T(8,128)(2,1)}, bf16[1792,512]{1,0:T(8,128)(2,1)S(1)}, u32[]{:S(2)}, u32[]{:S(2)}) collective-permute-start(bf16[1792,512]{1,0:T(8,128)(2,1)} %pad_maximum_fusion.4), channel_id=1, source_target_pairs={{0,2},{1,3},{2,0},{3,1},{4,6},{5,7},{6,4},{7,5},{8,10},{9,11},{10,... | collective-permute-start | bytes 5505032 | tf_op jit(solution)/shard_map/ppermute | solution.py:25
  171.9 125.7 %collective-permute-start.23 = (bf16[256,1792]{1,0:T(8,128)(2,1)}, bf16[256,1792]{1,0:T(8,128)(2,1)S(1)}, u32[]{:S(2)}, u32[]{:S(2)}) collective-permute-start(bf16[256,1792]{1,0:T(8,128)(2,1)} %get-tuple-element.8), channel_id=1, source_target_pairs={{0,2},{1,3},{2,0},{3,1},{4,6},{5,7},{6,4},{7,5},{8,10},{9,11},{10,... | collective-permute-start | bytes 2752520 | tf_op jit(solution)/shard_map/ppermute | solution.py:25
  172.4 125.7 %collective-permute-start.24 = (bf16[256,1792]{1,0:T(8,128)(2,1)}, bf16[256,1792]{1,0:T(8,128)(2,1)S(1)}, u32[]{:S(2)}, u32[]{:S(2)}) collective-permute-start(bf16[256,1792]{1,0:T(8,128)(2,1)} %get-tuple-element.10), channel_id=1, source_target_pairs={{0,1},{1,0},{2,3},{3,2},{4,5},{5,4},{6,7},{7,6},{8,9},{9,8},{10,11... | collective-permute-start | bytes 2752520 | tf_op jit(solution)/shard_map/ppermute | solution.py:25
  172.5 12.9 %collective-permute-start.11 = (bf16[128,1792]{1,0:T(8,128)(2,1)S(1)}, bf16[128,1792]{1,0:T(8,128)(2,1)S(1)}, u32[]{:S(2)}, u32[]{:S(2)}) collective-permute-start(bf16[128,1792]{1,0:T(8,128)(2,1)S(1)} %collective-permute-done.10), channel_id=1, source_target_pairs={{0,4},{4,0},{8,12},{12,8},{16,20},{20,16},{24,28},{28,24},{1,5},{5... | collective-permute-start | bytes 1376264 | tf_op jit(solution)/shard_map/ppermute | solution.py:25
  178.4 11.4 %collective-permute-start.49 = (bf16[256,1024]{1,0:T(8,128)(2,1)S(1)}, bf16[256,1024]{1,0:T(8,128)(2,1)S(1)}, u32[]{:S(2)}, u32[]{:S(2)}) collective-permute-start(bf16[256,1024]{1,0:T(8,128)(2,1)S(1)} %pad_maximum_fusion.9), channel_id=1, source_target_pairs={{0,1},{1,0},{2,3},{3,2},{4,5},{5,4},{6,7},{7,6},{8,9},{9,8},{10,11... | collective-permute-start | bytes 1572872 | tf_op jit(solution)/shard_map/ppermute | solution.py:25
  185.4 30.4 %collective-permute-start.28 = (bf16[128,1792]{1,0:T(8,128)(2,1)S(1)}, bf16[128,1792]{1,0:T(8,128)(2,1)S(1)}, u32[]{:S(2)}, u32[]{:S(2)}) collective-permute-start(bf16[128,1792]{1,0:T(8,128)(2,1)S(1)} %collective-permute-done.10), channel_id=1, source_target_pairs={{0,8},{4,12},{8,16},{12,20},{16,24},{20,28},{24,0},{28,4},{1,9},{5... | collective-permute-start | bytes 1376264 | tf_op jit(solution)/shard_map/ppermute | solution.py:25
  189.8 109.8 %collective-permute-start.25 = (bf16[256,1792]{1,0:T(8,128)(2,1)S(1)}, bf16[256,1792]{1,0:T(8,128)(2,1)S(1)}, u32[]{:S(2)}, u32[]{:S(2)}) collective-permute-start(bf16[256,1792]{1,0:T(8,128)(2,1)S(1)} %copy-done.9), channel_id=1, source_target_pairs={{0,3},{1,2},{2,1},{3,0},{4,7},{5,6},{6,5},{7,4},{8,11},{9,10},{10,... | collective-permute-start | bytes 2752520 | tf_op jit(solution)/shard_map/ppermute | solution.py:25
  214.2 36.9 %collective-permute-start.50 = (bf16[256,512]{1,0:T(8,128)(2,1)S(1)}, bf16[256,512]{1,0:T(8,128)(2,1)S(1)}, u32[]{:S(2)}, u32[]{:S(2)}) collective-permute-start(bf16[256,512]{1,0:T(8,128)(2,1)S(1)} %fusion.45), channel_id=1, source_target_pairs={{0,2},{1,3},{2,0},{3,1},{4,6},{5,7},{6,4},{7,5},{8,10},{9,11},{10,... | collective-permute-start | bytes 786440 | tf_op jit(solution)/shard_map/ppermute | solution.py:25
  215.8 48.1 %collective-permute-start.14 = (bf16[256,1024]{1,0:T(8,128)(2,1)S(1)}, bf16[256,1024]{1,0:T(8,128)(2,1)S(1)}, u32[]{:S(2)}, u32[]{:S(2)}) collective-permute-start(bf16[256,1024]{1,0:T(8,128)(2,1)S(1)} %pad_maximum_fusion.6), channel_id=1, source_target_pairs={{0,1},{1,0},{2,3},{3,2},{4,5},{5,4},{6,7},{7,6},{8,9},{9,8},{10,11... | collective-permute-start | bytes 1572872 | tf_op jit(solution)/shard_map/ppermute | solution.py:25
  251.0 8.5 %collective-permute-start.29 = (bf16[128,1792]{1,0:T(8,128)(2,1)S(1)}, bf16[128,1792]{1,0:T(8,128)(2,1)S(1)}, u32[]{:S(2)}, u32[]{:S(2)}) collective-permute-start(bf16[128,1792]{1,0:T(8,128)(2,1)S(1)} %collective-permute-done.28), channel_id=1, source_target_pairs={{0,4},{4,0},{8,12},{12,8},{16,20},{20,16},{24,28},{28,24},{1,5},{5... | collective-permute-start | bytes 1376264 | tf_op jit(solution)/shard_map/ppermute | solution.py:25
  259.5 11.0 %collective-permute-start.38 = (bf16[128,1792]{1,0:T(8,128)(2,1)S(1)}, bf16[128,1792]{1,0:T(8,128)(2,1)S(1)}, u32[]{:S(2)}, u32[]{:S(2)}) collective-permute-start(bf16[128,1792]{1,0:T(8,128)(2,1)S(1)} %collective-permute-done.28), channel_id=1, source_target_pairs={{0,8},{4,12},{8,16},{12,20},{16,24},{20,28},{24,0},{28,4},{1,9},{5... | collective-permute-start | bytes 1376264 | tf_op jit(solution)/shard_map/ppermute | solution.py:25
  263.9 5.0 %collective-permute-start.52 = (bf16[256,256]{1,0:T(8,128)(2,1)S(1)}, bf16[256,256]{1,0:T(8,128)(2,1)S(1)}, u32[]{:S(2)}, u32[]{:S(2)}) collective-permute-start(bf16[256,256]{1,0:T(8,128)(2,1)S(1)} %fusion.81), channel_id=1, source_target_pairs={{0,2},{1,3},{2,0},{3,1},{4,6},{5,7},{6,4},{7,5},{8,10},{9,11},{10,... | collective-permute-start | bytes 393224 | tf_op jit(solution)/shard_map/ppermute | solution.py:25
  269.0 6.4 %collective-permute-start.16 = (bf16[256,512]{1,0:T(8,128)(2,1)S(1)}, bf16[256,512]{1,0:T(8,128)(2,1)S(1)}, u32[]{:S(2)}, u32[]{:S(2)}) collective-permute-start(bf16[256,512]{1,0:T(8,128)(2,1)S(1)} %fusion.50), channel_id=1, source_target_pairs={{0,2},{1,3},{2,0},{3,1},{4,6},{5,7},{6,4},{7,5},{8,10},{9,11},{10,... | collective-permute-start | bytes 786440 | tf_op jit(solution)/shard_map/ppermute | solution.py:25
  270.5 17.0 %collective-permute-start.30 = (bf16[256,1024]{1,0:T(8,128)(2,1)S(1)}, bf16[256,1024]{1,0:T(8,128)(2,1)S(1)}, u32[]{:S(2)}, u32[]{:S(2)}) collective-permute-start(bf16[256,1024]{1,0:T(8,128)(2,1)S(1)} %pad_maximum_fusion.7), channel_id=1, source_target_pairs={{0,1},{1,0},{2,3},{3,2},{4,5},{5,4},{6,7},{7,6},{8,9},{9,8},{10,11... | collective-permute-start | bytes 1572872 | tf_op jit(solution)/shard_map/ppermute | solution.py:25
  275.3 8.5 %collective-permute-start.39 = (bf16[128,1792]{1,0:T(8,128)(2,1)S(1)}, bf16[128,1792]{1,0:T(8,128)(2,1)S(1)}, u32[]{:S(2)}, u32[]{:S(2)}) collective-permute-start(bf16[128,1792]{1,0:T(8,128)(2,1)S(1)} %collective-permute-done.38), channel_id=1, source_target_pairs={{0,4},{4,0},{8,12},{12,8},{16,20},{20,16},{24,28},{28,24},{1,5},{5... | collective-permute-start | bytes 1376264 | tf_op jit(solution)/shard_map/ppermute | solution.py:25
  283.8 7.2 %collective-permute-start.21 = (bf16[256,256]{1,0:T(8,128)(2,1)S(1)}, bf16[256,256]{1,0:T(8,128)(2,1)S(1)}, u32[]{:S(2)}, u32[]{:S(2)}) collective-permute-start(bf16[256,256]{1,0:T(8,128)(2,1)S(1)} %fusion.84), channel_id=1, source_target_pairs={{0,2},{1,3},{2,0},{3,1},{4,6},{5,7},{6,4},{7,5},{8,10},{9,11},{10,... | collective-permute-start | bytes 393224 | tf_op jit(solution)/shard_map/ppermute | solution.py:25
  288.3 6.4 %collective-permute-start.31 = (bf16[256,512]{1,0:T(8,128)(2,1)S(1)}, bf16[256,512]{1,0:T(8,128)(2,1)S(1)}, u32[]{:S(2)}, u32[]{:S(2)}) collective-permute-start(bf16[256,512]{1,0:T(8,128)(2,1)S(1)} %fusion.49), channel_id=1, source_target_pairs={{0,2},{1,3},{2,0},{3,1},{4,6},{5,7},{6,4},{7,5},{8,10},{9,11},{10,... | collective-permute-start | bytes 786440 | tf_op jit(solution)/shard_map/ppermute | solution.py:25
  291.1 38.6 %collective-permute-start.53 = (bf16[256,512]{1,0:T(8,128)(2,1)S(1)}, bf16[256,512]{1,0:T(8,128)(2,1)S(1)}, u32[]{:S(2)}, u32[]{:S(2)}) collective-permute-start(bf16[256,512]{1,0:T(8,128)(2,1)S(1)} %pad_maximum_fusion.13), channel_id=1, source_target_pairs={{0,1},{1,0},{2,3},{3,2},{4,5},{5,4},{6,7},{7,6},{8,9},{9,8},{10,11... | collective-permute-start | bytes 786440 | tf_op jit(solution)/shard_map/ppermute | solution.py:25
  297.5 6.4 %collective-permute-start.34 = (bf16[256,256]{1,0:T(8,128)(2,1)S(1)}, bf16[256,256]{1,0:T(8,128)(2,1)S(1)}, u32[]{:S(2)}, u32[]{:S(2)}) collective-permute-start(bf16[256,256]{1,0:T(8,128)(2,1)S(1)} %fusion.83), channel_id=1, source_target_pairs={{0,2},{1,3},{2,0},{3,1},{4,6},{5,7},{6,4},{7,5},{8,10},{9,11},{10,... | collective-permute-start | bytes 393224 | tf_op jit(solution)/shard_map/ppermute | solution.py:25
  298.1 10.9 %collective-permute-start.41 = (bf16[256,512]{1,0:T(8,128)(2,1)S(1)}, bf16[256,512]{1,0:T(8,128)(2,1)S(1)}, u32[]{:S(2)}, u32[]{:S(2)}) collective-permute-start(bf16[256,512]{1,0:T(8,128)(2,1)S(1)} %fusion.48), channel_id=1, source_target_pairs={{0,2},{1,3},{2,0},{3,1},{4,6},{5,7},{6,4},{7,5},{8,10},{9,11},{10,... | collective-permute-start | bytes 786440 | tf_op jit(solution)/shard_map/ppermute | solution.py:25
  300.8 12.3 %collective-permute-start.26 = (bf16[128,1792]{1,0:T(8,128)(2,1)S(1)}, bf16[128,1792]{1,0:T(8,128)(2,1)S(1)}, u32[]{:S(2)}, u32[]{:S(2)}) collective-permute-start(bf16[128,1792]{1,0:T(8,128)(2,1)S(1)} %slice.244), channel_id=1, source_target_pairs={{0,4},{4,0},{8,12},{12,8},{16,20},{20,16},{24,28},{28,24},{1,5},{5... | collective-permute-start | bytes 1376264 | tf_op jit(solution)/shard_map/ppermute | solution.py:25
  303.9 10.9 %collective-permute-start.35 = (bf16[256,512]{1,0:T(8,128)(2,1)S(1)}, bf16[256,512]{1,0:T(8,128)(2,1)S(1)}, u32[]{:S(2)}, u32[]{:S(2)}) collective-permute-start(bf16[256,512]{1,0:T(8,128)(2,1)S(1)} %pad_maximum_fusion.11), channel_id=1, source_target_pairs={{0,1},{1,0},{2,3},{3,2},{4,5},{5,4},{6,7},{7,6},{8,9},{9,8},{10,11... | collective-permute-start | bytes 786440 | tf_op jit(solution)/shard_map/ppermute | solution.py:25
  309.7 5.0 %collective-permute-start.44 = (bf16[256,256]{1,0:T(8,128)(2,1)S(1)}, bf16[256,256]{1,0:T(8,128)(2,1)S(1)}, u32[]{:S(2)}, u32[]{:S(2)}) collective-permute-start(bf16[256,256]{1,0:T(8,128)(2,1)S(1)} %fusion.82), channel_id=1, source_target_pairs={{0,2},{1,3},{2,0},{3,1},{4,6},{5,7},{6,4},{7,5},{8,10},{9,11},{10,... | collective-permute-start | bytes 393224 | tf_op jit(solution)/shard_map/ppermute | solution.py:25
  313.2 13.5 %collective-permute-start.27 = (bf16[128,1792]{1,0:T(8,128)(2,1)S(1)}, bf16[128,1792]{1,0:T(8,128)(2,1)S(1)}, u32[]{:S(2)}, u32[]{:S(2)}) collective-permute-start(bf16[128,1792]{1,0:T(8,128)(2,1)S(1)} %fusion.38), channel_id=1, source_target_pairs={{0,8},{4,12},{8,16},{12,20},{16,24},{20,28},{24,0},{28,4},{1,9},{5... | collective-permute-start | bytes 1376264 | tf_op jit(solution)/shard_map/ppermute | solution.py:25
  316.1 13.4 %collective-permute-start.36 = (bf16[128,1792]{1,0:T(8,128)(2,1)S(1)}, bf16[128,1792]{1,0:T(8,128)(2,1)S(1)}, u32[]{:S(2)}, u32[]{:S(2)}) collective-permute-start(bf16[128,1792]{1,0:T(8,128)(2,1)S(1)} %slice.243), channel_id=1, source_target_pairs={{0,4},{4,0},{8,12},{12,8},{16,20},{20,16},{24,28},{28,24},{1,5},{5... | collective-permute-start | bytes 1376264 | tf_op jit(solution)/shard_map/ppermute | solution.py:25
  318.8 20.5 %collective-permute-start.46 = (bf16[128,1792]{1,0:T(8,128)(2,1)S(1)}, bf16[128,1792]{1,0:T(8,128)(2,1)S(1)}, u32[]{:S(2)}, u32[]{:S(2)}) collective-permute-start(bf16[128,1792]{1,0:T(8,128)(2,1)S(1)} %slice.242), channel_id=1, source_target_pairs={{0,4},{4,0},{8,12},{12,8},{16,20},{20,16},{24,28},{28,24},{1,5},{5... | collective-permute-start | bytes 1376264 | tf_op jit(solution)/shard_map/ppermute | solution.py:25
  329.6 13.9 %collective-permute-start.37 = (bf16[128,1792]{1,0:T(8,128)(2,1)S(1)}, bf16[128,1792]{1,0:T(8,128)(2,1)S(1)}, u32[]{:S(2)}, u32[]{:S(2)}) collective-permute-start(bf16[128,1792]{1,0:T(8,128)(2,1)S(1)} %fusion.37), channel_id=1, source_target_pairs={{0,8},{4,12},{8,16},{12,20},{16,24},{20,28},{24,0},{28,4},{1,9},{5... | collective-permute-start | bytes 1376264 | tf_op jit(solution)/shard_map/ppermute | solution.py:25
  330.8 17.9 %collective-permute-start.54 = (bf16[128,1792]{1,0:T(8,128)(2,1)S(1)}, bf16[128,1792]{1,0:T(8,128)(2,1)S(1)}, u32[]{:S(2)}, u32[]{:S(2)}) collective-permute-start(bf16[128,1792]{1,0:T(8,128)(2,1)S(1)} %slice.241), channel_id=1, source_target_pairs={{0,4},{4,0},{8,12},{12,8},{16,20},{20,16},{24,28},{28,24},{1,5},{5... | collective-permute-start | bytes 1376264 | tf_op jit(solution)/shard_map/ppermute | solution.py:25
  343.6 13.0 %collective-permute-start.47 = (bf16[128,1792]{1,0:T(8,128)(2,1)S(1)}, bf16[128,1792]{1,0:T(8,128)(2,1)S(1)}, u32[]{:S(2)}, u32[]{:S(2)}) collective-permute-start(bf16[128,1792]{1,0:T(8,128)(2,1)S(1)} %fusion.35), channel_id=1, source_target_pairs={{0,8},{4,12},{8,16},{12,20},{16,24},{20,28},{24,0},{28,4},{1,9},{5... | collective-permute-start | bytes 1376264 | tf_op jit(solution)/shard_map/ppermute | solution.py:25
  (21 other events, 209.0 us)

commit v2 on v1

--- a/solution.py
+++ b/solution.py
@@ -1,6 +1,10 @@
+import functools
+
 import jax
 import jax.numpy as jnp
 from jax import lax
+from jax.experimental import pallas as pl
+from jax.experimental.pallas import tpu as pltpu
 from jax.sharding import PartitionSpec as P
 
 NOPE = 128
@@ -9,6 +13,7 @@
 TOP = 4
 CORES = 2
 DEPTH = 4
+META = 128
 
 
 EPS = 1e-06
@@ -77,24 +82,13 @@
     keys = jnp.concatenate([latent_kv, key_rope], axis=0)
     key_blocks = gather_ctx(keys)
 
-    gate_up = {}
-    down = {}
-    for dy in range(ny):
-        for dc in range(nc):
-            begin = tp_at(dy, dc) * col_width
-            piece = jnp.concatenate(
-                [
-                    lax.dynamic_slice_in_dim(gate_proj[0], begin, col_width, 0),
-                    lax.dynamic_slice_in_dim(up_proj[0], begin, col_width, 0),
-                ],
-                axis=1,
-            )
-            gate_up[dy, dc] = over_tp(piece, dy, dc) if (dy or dc) else piece
-    for dy in range(ny):
-        for dc in range(nc):
-            begin = tp_at(dy, dc) * col_width
-            piece = lax.dynamic_slice_in_dim(down_proj[0], begin, col_width, 1)
-            down[dy, dc] = over_tp(piece, dy, dc) if (dy or dc) else piece
+    def exchanged(weight, dy, dc):
+        piece = lax.dynamic_slice_in_dim(weight[0], tp_at(dy, dc) * col_width, col_width, 0)
+        return over_tp(piece, dy, dc) if (dy or dc) else piece
+
+    offsets = [(dy, dc) for dc in range(nc) for dy in range(ny)]
+    gates = [exchanged(gate_proj, dy, dc) for dy, dc in offsets]
+    ups = [exchanged(up_proj, dy, dc) for dy, dc in offsets]
 
     query_pos = ctx * row_count + jnp.arange(row_count, dtype=jnp.int32)
     query_lat = jnp.einsum(
@@ -103,6 +97,7 @@
         absorb_key,
         preferred_element_type=jnp.float32,
     ).astype(jnp.bfloat16)
+    query_lat, *gates = lax.optimization_barrier((query_lat, *gates))
     query_rot = query_rope.reshape(row_count, head_count, ROPE)
     score_scale = (NOPE + ROPE) ** (-0.5)
     all_keys = jnp.concatenate([b for line in key_blocks for b in line], axis=1)
@@ -129,6 +124,7 @@
     heads_out = jnp.einsum(
         "thl,hlv->thv", attn_lat, absorb_value, preferred_element_type=jnp.float32
     ).astype(jnp.bfloat16)
+    heads_out, *ups = lax.optimization_barrier((heads_out, *ups))
     attn_part = jnp.dot(
         heads_out.reshape(row_count, head_count * VDIM),
         out_proj,
@@ -150,7 +146,6 @@
 
     gain = lax.dynamic_slice_in_dim(norm_gain, col_start, col_width, 0).astype(jnp.float32)
     scaled = residual * gain[None, :]
-    token_blocks = gather_ctx(scaled.astype(jnp.bfloat16))
 
     router_cols = lax.dynamic_slice_in_dim(router, col_start, col_width, 1).astype(jnp.float32)
     stats = jnp.concatenate(
@@ -162,8 +157,7 @@
         ],
         axis=0,
     )
-    for dc in range(1, nc):
-        stats = stats + over_tp(stats, 0, dc) if nc == 2 else stats
+    stats = sum([over_tp(stats, 0, dc) for dc in range(1, nc)], stats)
     stats = sum([over_tp(stats, dy, 0) for dy in range(1, ny)], stats)
     inv_rms = lax.rsqrt(stats[expert_count] / model_width + EPS)
     logits = stats[:expert_count] * inv_rms[None, :]
@@ -173,56 +167,293 @@
     gate_vals = jax.nn.sigmoid(chosen)
     gate_vals = ROUTE_SCALE * gate_vals / jnp.sum(gate_vals, axis=0, keepdims=True)
     dense_gates = jnp.sum(jnp.where(onehot, gate_vals[:, None, :], 0.0), axis=0)
-    meta_blocks = gather_ctx(jnp.concatenate([dense_gates, inv_rms[None, :]], axis=0))
-
-    down_mat = jnp.concatenate(
-        [down[dy, dc] for dc in range(nc) for dy in range(ny)], axis=0
-    )
-
-    def experts(dz):
-        rows = jnp.concatenate(token_blocks[dz], axis=0)
-        meta = jnp.concatenate(meta_blocks[dz], axis=1)
-        row_scale = meta[expert_count][:, None]
-        row_gate = lax.dynamic_slice_in_dim(meta, ctx, 1, 0)[0][:, None]
-
-        def product(dy, dc):
-            return jnp.dot(rows, gate_up[dy, dc], preferred_element_type=jnp.float32)
-
-        sums = [None] * ny
-        for dc in list(range(1, nc)):
-            away = jnp.concatenate(
-                [product(dy, dc).astype(jnp.bfloat16) for dy in range(ny)], axis=1
-            )
-            away = over_tp(away, 0, -dc).astype(jnp.float32)
+    tokens = (scaled * inv_rms[:, None]).astype(jnp.bfloat16)
+    high = dense_gates.T.astype(jnp.bfloat16)
+    low = (dense_gates.T - high.astype(jnp.float32)).astype(jnp.bfloat16)
+    fill = jnp.zeros((row_count, META // 2 - expert_count), jnp.bfloat16)
+    packet = jnp.concatenate([tokens, high, fill, low, fill], axis=1)
+    routed_sum = expert_call((nz, nx, ny, nc), packet, gates, ups, down_proj[0])
+    return (residual + routed_sum).astype(jnp.bfloat16)
+
+
+def expert_kernel(dims, *refs):
+    nz, nx, ny, nc = dims
+    n_tp = ny * nc
+    packet, refs = refs[0], refs[1:]
+    gates, ups, refs = refs[:n_tp], refs[n_tp : 2 * n_tp], refs[2 * n_tp :]
+    down, out = refs[0], refs[1]
+    (tok, dmat, own, core_out, core_in, y_out, y_in, hid, acc, x_out, x_in, z_out, z_in) = refs[2:15]
+    (s_z, r_z, s_x, r_x, s_d, r_d, s_c, r_c, s_y, r_y) = refs[15:25]
+    (s_hy, r_hy, s_hc, r_hc, s_bx, r_bx, s_bz, r_bz, local_sem) = refs[25:]
+    rows, width = out.shape
+    h = down.shape[0]
+    ctx, tp = lax.axis_index("ctx"), lax.axis_index("tp")
+    z, x, y, c = ctx // nx, ctx % nx, tp // nc, tp % nc
+
+    def ctx_at(dz, dx):
+        return ((z + dz + nz) % nz * nx + (x + dx + nx) % nx, tp)
+
+    def tp_at(dy, dc):
+        return (ctx, (y + dy + ny) % ny * nc + (c + dc + nc) % nc)
+
+    def push(src, dst, send, recv, where):
+        copy = pltpu.make_async_remote_copy(
+            src_ref=src,
+            dst_ref=dst,
+            send_sem=send,
+            recv_sem=recv,
+            device_id=where,
+            device_id_type=pl.DeviceIdType.MESH,
+        )
+        copy.start()
+        return copy
+
+    peers = [ctx_at(0, dx) for dx in range(1, nx)]
+    if nz > 1:
+        peers.append(ctx_at(1, 0))
+    if nz > 2:
+        peers.append(ctx_at(-1, 0))
+    peers += [tp_at(dy, dc) for dc in range(nc) for dy in range(ny) if dy or dc]
+    barrier = pltpu.get_barrier_semaphore()
+    for peer in peers:
+        pl.semaphore_signal(
+            barrier, inc=1, device_id=peer, device_id_type=pl.DeviceIdType.MESH
+        )
+    pl.semaphore_wait(barrier, len(peers))
+
+    sent = []
+    zc, xc, dcp, cc, yc, hyc, hcc, bxc, bzc = ({} for _ in range(9))
+
+    def pass_on(dz):
+        block = packet if dz == 0 else tok.at[dz, pl.ds(0, rows)]
+        if dz:
+            zc[dz].wait_recv()
+        if dz + 1 < nz:
+            zc[dz + 1] = push(
+                block, tok.at[dz + 1, pl.ds(0, rows)], s_z.at[dz], r_z.at[dz], ctx_at(1, 0)
+            )
+            sent.append(zc[dz + 1])
+        for dx in range(1, nx):
+            xc[dz, dx] = push(
+                block,
+                tok.at[dz, pl.ds(dx * rows, rows)],
+                s_x.at[dz, dx - 1],
+                r_x.at[dz, dx - 1],
+                ctx_at(0, dx),
+            )
+            sent.append(xc[dz, dx])
+
+    def down_cols(dy, dc):
+        begin = tp_at(dy, dc)[1] * width
+        return down.at[:, pl.ds(pl.multiple_of(begin, 128), width)]
+
+    pass_on(0)
+    mine = pltpu.make_async_copy(down_cols(0, 0), dmat.at[pl.ds(0, h)], local_sem)
+    mine.start()
+    for dc in range(nc - 1, -1, -1):
+        for dy in range(ny):
+            if dy or dc:
+                k = dc * ny + dy
+                dcp[k] = push(
+                    down_cols(dy, dc),
+                    dmat.at[pl.ds(k * h, h)],
+                    s_d.at[k - 1],
+                    r_d.at[k - 1],
+                    tp_at(dy, dc),
+                )
+                sent.append(dcp[k])
+    tok[0, pl.ds(0, rows), :] = packet[...]
+
+    def products(dz):
+        for dx in range(1, nx):
+            xc[dz, dx].wait_recv()
+        for dc in range(nc - 1, -1, -1):
             for dy in range(ny):
-                term = away[:, dy * 2 * hid : (dy + 1) * 2 * hid]
-                sums[dy] = term if sums[dy] is None else sums[dy] + term
-        for dy in range(ny):
-            mine = product(dy, 0)
-            sums[dy] = mine if sums[dy] is None else sums[dy] + mine
-        total = sums[0]
+                k = dc * ny + dy
+                for part, weight in enumerate((gates[k], ups[k])):
+                    value = jnp.dot(
+                        tok[dz, :, pl.ds(0, width)],
+                        weight[...],
+                        preferred_element_type=jnp.float32,
+                    )
+                    if dc:
+                        lanes = pl.ds((2 * dy + part) * h, h)
+                        core_out[dz, dc - 1, :, lanes] = value.astype(jnp.bfloat16)
+                    else:
+                        own[dz, dy, :, pl.ds(part * h, h)] = value
+            if dc:
+                cc[dz, dc] = push(
+                    core_out.at[dz, dc - 1],
+                    core_in.at[dz, dc - 1],
+                    s_c.at[dz, dc - 1],
+                    r_c.at[dz, dc - 1],
+                    tp_at(0, -dc),
+                )
+                sent.append(cc[dz, dc])
+
+    def chip_sums(dz):
+        for dc in range(1, nc):
+            cc[dz, dc].wait_recv()
+        for dy in list(range(1, ny)) + [0]:
+            value = own[dz, dy]
+            for dc in range(1, nc):
+                value = value + core_in[dz, dc - 1, :, pl.ds(2 * dy * h, 2 * h)].astype(jnp.float32)
+            if dy:
+                y_out[dz, dy - 1] = value.astype(jnp.bfloat16)
+                yc[dz, dy] = push(
+                    y_out.at[dz, dy - 1],
+                    y_in.at[dz, dy - 1],
+                    s_y.at[dz, dy - 1],
+                    r_y.at[dz, dy - 1],
+                    tp_at(-dy, 0),
+                )
+                sent.append(yc[dz, dy])
+            else:
+                own[dz, 0] = value
+
+    def activate(dz):
+        value = own[dz, 0]
         for dy in range(1, ny):
-            total = total + over_tp(sums[dy].astype(jnp.bfloat16), -dy, 0).astype(jnp.float32)
-        total = total * row_scale
-        hidden = (jax.nn.silu(total[:, :hid]) * total[:, hid:]).astype(jnp.bfloat16)
-        line = jnp.concatenate(
-            [hidden] + [over_tp(hidden, dy, 0) for dy in range(1, ny)], axis=1
-        )
-        whole = jnp.concatenate([line] + [over_tp(line, 0, dc) for dc in range(1, nc)], axis=1)
-        out = jnp.dot(whole, down_mat, preferred_element_type=jnp.float32) * row_gate
-        acc = out[:row_count]
+            yc[dz, dy].wait_recv()
+            value = value + y_in[dz, dy - 1].astype(jnp.float32)
+        gate, up = value[:, :h], value[:, h:]
+        hid[dz, :, pl.ds(0, h)] = (gate / (1.0 + jnp.exp(-gate)) * up).astype(jnp.bfloat16)
+        for dy in range(1, ny):
+            hyc[dz, dy] = push(
+                hid.at[dz, :, pl.ds(0, h)],
+                hid.at[dz, :, pl.ds(dy * h, h)],
+                s_hy.at[dz, dy - 1],
+                r_hy.at[dz, dy - 1],
+                tp_at(dy, 0),
+            )
+            sent.append(hyc[dz, dy])
+
+    def share_hidden(dz):
+        for dy in range(1, ny):
+            hyc[dz, dy].wait_recv()
+        for dc in range(1, nc):
+            hcc[dz, dc] = push(
+                hid.at[dz, :, pl.ds(0, ny * h)],
+                hid.at[dz, :, pl.ds(dc * ny * h, ny * h)],
+                s_hc.at[dz, dc - 1],
+                r_hc.at[dz, dc - 1],
+                tp_at(0, dc),
+            )
+            sent.append(hcc[dz, dc])
+
+    step = 256 if width % 256 == 0 else 128
+
+    def outputs(dz, first):
+        for dc in range(1, nc):
+            hcc[dz, dc].wait_recv()
+        if first:
+            mine.wait()
+            for k in dcp:
+                dcp[k].wait_recv()
+        meta = tok[dz, :, pl.ds(width, META)].astype(jnp.float32)
+        lane = lax.broadcasted_iota(jnp.int32, meta.shape, 1)
+        picked = (lane == ctx) | (lane == ctx + META // 2)
+        gate = jnp.sum(jnp.where(picked, meta, 0.0), axis=1, keepdims=True)
+        for j in range(width // step):
+            cols = pl.ds(j * step, step)
+            value = gate * jnp.dot(
+                hid[dz], dmat[:, cols], preferred_element_type=jnp.float32
+            )
+            acc[dz, :, cols] = value[:rows]
+            for dx in range(1, nx):
+                x_out[dz, dx - 1, :, cols] = value[dx * rows : (dx + 1) * rows].astype(jnp.bfloat16)
         for dx in range(1, nx):
-            other = out[dx * row_count : (dx + 1) * row_count].astype(jnp.bfloat16)
-            acc = acc + over_ctx(other, 0, -dx).astype(jnp.float32)
-        return acc
-
-    parts = [experts(dz) for dz in range(nz)]
-    total = None
-    for dz in list(range(1, nz)):
-        total = parts[dz] if total is None else total + parts[dz]
-        total = over_ctx(total.astype(jnp.bfloat16), 1, 0).astype(jnp.float32)
-    routed_sum = parts[0] if total is None else total + parts[0]
-    return (residual + routed_sum).astype(jnp.bfloat16)
+            bxc[dz, dx] = push(
+                x_out.at[dz, dx - 1],
+                x_in.at[dz, dx - 1],
+                s_bx.at[dz, dx - 1],
+                r_bx.at[dz, dx - 1],
+                ctx_at(0, -dx),
+            )
+            sent.append(bxc[dz, dx])
+
+    def give_back(dz):
+        value = acc[dz]
+        for dx in range(1, nx):
+            bxc[dz, dx].wait_recv()
+            value = value + x_in[dz, dx - 1].astype(jnp.float32)
+        if dz != 1 and nz > 1:
+            before = (dz or nz) - 1
+            bzc[before].wait_recv()
+            value = value + z_in[before - 1].astype(jnp.float32)
+        if dz:
+            z_out[dz - 1] = value.astype(jnp.bfloat16)
+            bzc[dz] = push(
+                z_out.at[dz - 1], z_in.at[dz - 1], s_bz.at[dz - 1], r_bz.at[dz - 1], ctx_at(1, 0)
+            )
+            sent.append(bzc[dz])
+        else:
+            out[...] = value
+
+    for turn in range(nz + 3):
+        if turn + 1 < nz:
+            pass_on(turn + 1)
+        if turn < nz:
+            products(turn)
+        if 0 <= turn - 1 < nz:
+            chip_sums(turn - 1)
+        if 0 <= turn - 2 < nz:
+            share_hidden(turn - 2)
+        if 0 <= turn - 1 < nz:
+            activate(turn - 1)
+        if 0 <= turn - 2 < nz:
+            outputs(turn - 2, turn == 2)
+        if 1 <= turn - 3 < nz:
+            give_back(turn - 3)
+    give_back(0)
+    for copy in sent:
+        copy.wait_send()
+
+
+def expert_call(dims, packet, gates, ups, down):
+    nz, nx, ny, nc = dims
+    n_tp = ny * nc
+    rows = packet.shape[0]
+    width = packet.shape[1] - META
+    h = down.shape[0]
+    all_rows = nx * rows
+    px, py, pc, pz = max(nx - 1, 1), max(ny - 1, 1), max(nc - 1, 1), max(nz - 1, 1)
+    bf16, f32 = jnp.bfloat16, jnp.float32
+    vmem = pl.BlockSpec(memory_space=pltpu.VMEM)
+    sem = pltpu.SemaphoreType.DMA
+    shapes = [
+        pltpu.VMEM((nz, all_rows, width + META), bf16),
+        pltpu.VMEM((n_tp * h, width), bf16),
+        pltpu.VMEM((nz, ny, all_rows, 2 * h), f32),
+        pltpu.VMEM((nz, pc, all_rows, ny * 2 * h), bf16),
+        pltpu.VMEM((nz, pc, all_rows, ny * 2 * h), bf16),
+        pltpu.VMEM((nz, py, all_rows, 2 * h), bf16),
+        pltpu.VMEM((nz, py, all_rows, 2 * h), bf16),
+        pltpu.VMEM((nz, all_rows, n_tp * h), bf16),
+        pltpu.VMEM((nz, rows, width), f32),
+        pltpu.VMEM((nz, px, rows, width), bf16),
+        pltpu.VMEM((nz, px, rows, width), bf16),
+        pltpu.VMEM((pz, rows, width), bf16),
+        pltpu.VMEM((pz, rows, width), bf16),
+    ]
+    sems = []
+    for shape in ((pz,), (nz, px), (n_tp,), (nz, pc), (nz, py), (nz, py), (nz, pc), (nz, px), (pz,)):
+        sems += [sem(shape), sem(shape)]
+    flops = 2 * nz * all_rows * width * n_tp * h * 3
+    return pl.pallas_call(
+        functools.partial(expert_kernel, dims),
+        out_shape=jax.ShapeDtypeStruct((rows, width), f32),
+        in_specs=[vmem] * (1 + 2 * n_tp) + [pl.BlockSpec(memory_space=pl.ANY)],
+        out_specs=vmem,
+        scratch_shapes=shapes + sems + [sem],
+        compiler_params=pltpu.CompilerParams(
+            collective_id=1, has_side_effects=True, vmem_limit_bytes=58 * 1024 * 1024
+        ),
+        cost_estimate=pl.CostEstimate(
+            flops=flops, bytes_accessed=16 * 1024 * 1024, transcendentals=0
+        ),
+        name="experts",
+    )(packet, *gates, *ups, down)
 
 
 def solution(mesh):

time: 358 us -> 247 us (0.69)
  waiting for transfers between devices: 222 us -> 52.4 us
  Pallas kernels: 0 us -> 117 us
  matrix products: 64.5 us -> 37.9 us
  starting transfers between devices: 40.1 us -> 18.2 us
  other arithmetic: 13 us -> 5.48 us
    ppermute x55 -> x18, waiting for transfers between devices: 222 us -> 52.4 us  [move(): return lax.ppermute(value, axis, pairs)]
    pallas_call x0 -> x1, Pallas kernels: none -> 117 us  [expert_call(): pl.pallas_call(functools.partial(expert_kernel, dims), out_shape=jax.Shap...]
    dot_general x20 -> x1, matrix products: 26.7 us -> 2.12 us  [body(): jnp.einsum('thn,hnl->thl', query_nope.reshape(row_count, head_count, NOPE...]
    ppermute x55 -> x18, starting transfers between devices: 40.1 us -> 18.2 us  [move(): return lax.ppermute(value, axis, pairs)]
    concatenate x13 -> x0, other arithmetic: 4.52 us -> none  [the longest x3 4.22 us: body(): jnp.concatenate([lax.dynamic_slice_in_dim(gate_proj[0], begin, col_width,...]
    unnamed x42 -> x26, local copies, waits for them, and re-layouts: 7.67 us -> 4.71 us
  transfers between devices with their start and end apart: 55 -> 18, of which waited for: 32 -> 10; matrix products, arithmetic and copies ran while one was open for 14% -> 15% of each run, Pallas kernels for 0% -> 0%
where the time goes in v2:
time: 247 us; the launch traced here: 246 us
  Pallas kernels  117 us (47%)
  waiting for transfers between devices  52.4 us (21%)
  matrix products  37.9 us (15%)
  starting transfers between devices  18.2 us (7%)
  local copies, waits for them, and re-layouts  15.5 us (6%)
  other arithmetic  5.48 us (2%)
    pallas_call x1, Pallas kernels, expert_call(): pl.pallas_call(functools.partial(expert_kernel, dims), out_shape=jax.Shap...  117 us
    ppermute x18, waiting for transfers between devices, move(): return lax.ppermute(value, axis, pairs)  52.4 us
    ppermute x18, starting transfers between devices, move(): return lax.ppermute(value, axis, pairs)  18.2 us
    sub x1, matrix products, body(): scores - top_score[:, :, None]  11.6 us
    dot_general x1, matrix products, body(): jnp.dot(heads_out.reshape(row_count, head_count * VDIM), out_proj, prefer...  11.5 us
    dynamic_slice x2, local copies, waits for them, and re-layouts, exchanged(): lax.dynamic_slice_in_dim(weight[0], tp_at(dy, dc) * col_width, col_width, 0)  7.85 us
    dot_general x1, matrix products, body(): jnp.einsum('thl,hlv->thv', attn_lat, absorb_value, preferred_element_type...  5.8 us
    dot_general x1, matrix products, body(): jnp.einsum('thl,ls->ths', query_lat, latent, preferred_element_type=jnp.f...  5.6 us
  transfers between devices with their start and end apart: 18, of which 10 were waited for; matrix products, arithmetic and copies ran while one was open for 15% of the time, Pallas kernels for 0%

profile of v2, /device:TPU:0, one launch (start us, length us, event | category | flops | bytes accessed | tf_op | source)
XLA Modules:
  0.0 246.3 jit_solution(552498985652146025)
XLA Ops:
  0.0 1.7 constant_dynamic-update-slice_fusion.1
  1.7 1.3 constant_dynamic-update-slice_fusion
  3.1 2.9 %collective-permute-start.3 = (bf16[576,128]{1,0:T(8,128)(2,1)}, bf16[576,128]{1,0:T(8,128)(2,1)}, u32[]{:S(2)}, u32[]{:S(2)}) collective-permute-start(bf16[576,128]{1,0:T(8,128)(2,1)} %get-tuple-element.41), channel_id=1, source_target_pairs={{0,4},{4,0},{8,12},{12,8},{16,20},{20,16},{24,28},{28,24},{1,5},{5... | collective-permute-start | bytes 442376 | tf_op jit(solution)/shard_map/ppermute | solution.py:30
  6.0 1.6 collective-permute-start.4
  7.6 3.9 %dynamic-slice_bitcast_fusion.4 = (bf16[1792,256]{1,0:T(8,128)(2,1)}, bf16[1792,256]{1,0:T(8,128)(2,1)}, bf16[1792,256]{1,0:T(8,128)(2,1)}, bf16[1792,256]{1,0:T(8,128)(2,1)}) fusion(bf16[1,7168,256]{2,1,0:T(8,128)(2,1)} %param.25, s32[]{:T(128)S(6)} %select_n.174, s32[]{:T(128)S(6)} %select_n.171, s32[]{:T(128)S(6)} %select_n.169, s32[]{:T(128)S(6)} %select_n.173), kind=kLoop, calls=%fused_computation.28 | loop fusion | bytes 7340048 | tf_op jit(solution)/shard_map/dynamic_slice | solution.py:86
  11.5 1.5 collective-permute-start
  13.0 0.6 collective-permute-start.2
  13.8 4.0 %dynamic-slice_bitcast_fusion = (bf16[1792,256]{1,0:T(8,128)(2,1)}, bf16[1792,256]{1,0:T(8,128)(2,1)}, bf16[1792,256]{1,0:T(8,128)(2,1)}, bf16[1792,256]{1,0:T(8,128)(2,1)}) fusion(bf16[1,7168,256]{2,1,0:T(8,128)(2,1)} %param.26, s32[]{:T(128)S(6)} %select_n.174, s32[]{:T(128)S(6)} %select_n.171, s32[]{:T(128)S(6)} %select_n.169, s32[]{:T(128)S(6)} %select_n.173), kind=kLoop, calls=%fused_computation.24 | loop fusion | bytes 7340048 | tf_op jit(solution)/shard_map/dynamic_slice | solution.py:86
  17.8 2.1 convert_bitcast_fusion
  19.9 0.8 broadcast_compare_fusion
  20.7 0.8 copy.36
  21.5 0.5 collective-permute-start.5
  22.1 1.6 collective-permute-start.6
  23.7 1.0 constant_dynamic-update-slice_fusion.8
  24.6 1.0 constant_dynamic-update-slice_fusion.7
  25.6 4.0 %collective-permute-done.6 = bf16[576,128]{1,0:T(8,128)(2,1)S(1)} collective-permute-done((bf16[576,128]{1,0:T(8,128)(2,1)}, bf16[576,128]{1,0:T(8,128)(2,1)S(1)}, u32[]{:S(2)}, u32[]{:S(2)}) %collective-permute-start.6) | collective-permute-done | bytes 147488 | tf_op jit(solution)/shard_map/ppermute | solution.py:30
  29.6 1.5 collective-permute-start.7
  31.2 3.5 %collective-permute-done.7 = bf16[576,128]{1,0:T(8,128)(2,1)S(1)} collective-permute-done((bf16[576,128]{1,0:T(8,128)(2,1)S(1)}, bf16[576,128]{1,0:T(8,128)(2,1)S(1)}, u32[]{:S(2)}, u32[]{:S(2)}) %collective-permute-start.7) | collective-permute-done | bytes 147488 | tf_op jit(solution)/shard_map/ppermute | solution.py:30
  34.7 1.5 collective-permute-start.10
  36.2 1.8 collective-permute-done.8
  38.0 0.5 collective-permute-start.9
  38.6 4.5 %collective-permute-done.9 = bf16[576,128]{1,0:T(8,128)(2,1)S(1)} collective-permute-done((bf16[576,128]{1,0:T(8,128)(2,1)S(1)}, bf16[576,128]{1,0:T(8,128)(2,1)S(1)}, u32[]{:S(2)}, u32[]{:S(2)}) %collective-permute-start.9) | collective-permute-done | bytes 147488 | tf_op jit(solution)/shard_map/ppermute | solution.py:30
  43.2 1.7 collective-permute-start.12
  44.9 8.9 %collective-permute-done.2.refs_4_ = bf16[1792,256]{1,0:T(8,128)(2,1)} collective-permute-done((bf16[1792,256]{1,0:T(8,128)(2,1)}, bf16[1792,256]{1,0:T(8,128)(2,1)}, u32[]{:S(2)}, u32[]{:S(2)}) %collective-permute-start.2) | collective-permute-done | bytes 917536 | tf_op jit(solution)/shard_map/ppermute | solution.py:30
  53.8 5.6 %fusion.25 = f32[128,16,1024]{2,0,1:T(8,128)} fusion(bf16[128,16,512]{0,2,1:T(8,128)(2,1)S(1)} %copy-done.3, bf16[576,1024]{1,0:T(8,128)(2,1)S(1)} %constant_dynamic-update-slice_fusion.2), kind=kOutput, calls=%fused_computation.34 | convolution fusion | flops 2147483648 | bytes 11534336 | tf_op jit(solution)/shard_map/thl,ls->ths/dot_general | solution.py:112
  59.4 11.6 %fusion.40 = (f32[128,16]{0,1:T(8,128)S(1)}, bf16[128,16,1024]{2,0,1:T(8,128)(2,1)}) fusion(pred[128,1024]{1,0:T(8,128)(4,1)} %broadcast_compare_fusion, f32[128,16,1024]{2,0,1:T(8,128)} %fusion.25, bf16[128,16,64]{0,2,1:T(8,128)(2,1)S(1)} %bitcast.90, bf16[576,1024]{1,0:T(8,128)(2,1)S(1)} %constant_dynamic-update-slice_fusion.2), kind=kOutput, calls=%fused_computation.76 | convolution fusion | flops 555746304 | bytes 22028288 | tf_op jit(solution)/shard_map/sub | solution.py:118
  71.0 5.8 %fusion.18 = bf16[128,16,128]{2,0,1:T(8,128)(2,1)S(1)} fusion(bf16[16,512,128]{2,1,0:T(8,128)(2,1)} %param.20, f32[128,16]{0,1:T(8,128)S(1)} %get-tuple-element.43, bf16[128,16,1024]{2,0,1:T(8,128)(2,1)} %get-tuple-element.44, bf16[576,1024]{1,0:T(8,128)(2,1)S(1)} %constant_dynamic-update-slice_fusion.2), kind=kOutput, calls=%fused_computation.14 | convolution fusion | flops 2418278400 | bytes 7872512 | tf_op jit(solution)/shard_map/thl,hlv->thv/dot_general | solution.py:124
  76.8 14.5 %collective-permute-done.12.refs_8_ = bf16[1792,256]{1,0:T(8,128)(2,1)} collective-permute-done((bf16[1792,256]{1,0:T(8,128)(2,1)}, bf16[1792,256]{1,0:T(8,128)(2,1)}, u32[]{:S(2)}, u32[]{:S(2)}) %collective-permute-start.12) | collective-permute-done | bytes 917536 | tf_op jit(solution)/shard_map/ppermute | solution.py:30
  91.3 0.3 copy.38
  91.6 11.5 %fusion.41 = f32[128,7168]{1,0:T(8,128)S(1)} fusion(bf16[128,2048]{0,1:T(8,128)(2,1)S(1)} %bitcast.89, bf16[2048,7168]{1,0:T(8,128)(2,1)} %param.21), kind=kOutput, calls=%fused_computation.77 | convolution fusion | flops 3758096384 | bytes 33554432 | tf_op jit(solution)/shard_map/dot_general | solution.py:128
  103.1 0.1 dynamic-slice_convert_fusion.1
  103.2 0.8 collective-permute-start.14
  104.2 1.4 collective-permute-done.14
  105.5 0.1 add_convert_fusion.1
  105.6 1.6 collective-permute-start.15
  107.2 0.8 dynamic-slice_convert_fusion.2
  108.0 10.5 %collective-permute-done.15 = bf16[128,1792]{1,0:T(8,128)(2,1)S(1)} collective-permute-done((bf16[128,1792]{1,0:T(8,128)(2,1)S(1)}, bf16[128,1792]{1,0:T(8,128)(2,1)S(1)}, u32[]{:S(2)}, u32[]{:S(2)}) %collective-permute-start.15) | collective-permute-done | bytes 458784 | tf_op jit(solution)/shard_map/ppermute | solution.py:30
  118.5 1.5 multiply_reduce_fusion
  120.0 1.3 fusion.23
  121.3 0.1 collective-permute-start.16
  121.4 1.2 collective-permute-done.16
  122.6 1.5 collective-permute-start.17
  124.1 2.1 collective-permute-done.17
  126.2 0.1 multiply_convert_fusion
  126.4 0.1 copy.39
  126.6 1.0 concatenate.19.refs_0_
  127.6 116.7 %experts.1 = f32[128,1792]{1,0:T(8,128)} custom-call(bf16[128,1920]{1,0:T(8,128)(2,1)} %concatenate.19.refs_0_, bf16[1792,256]{1,0:T(8,128)(2,1)} %get-tuple-element.17.refs_1_, bf16[1792,256]{1,0:T(8,128)(2,1)} %collective-permute-done.refs_2_, bf16[1792,256]{1,0:T(8,128)(2,1)} %collective-permute-done.1.refs_3_, ...), custom_call_target="tpu_custom_call" | custom-call | flops 11274289152 | bytes 16777216 | tf_op jit(solution)/shard_map/experts/pallas_call | solution.py:443
  244.2 2.0 add_convert_fusion
  (50 shorter events, 0.7 us)
Async XLA Ops:
  0.0 17.8 %copy-start = (bf16[16,128,512]{2,1,0:T(8,128)(2,1)S(1)}, bf16[16,128,512]{2,1,0:T(8,128)(2,1)}, u32[]{:S(2)}) copy-start(bf16[16,128,512]{2,1,0:T(8,128)(2,1)} %param.19) | copy-start | bytes 6291460
  3.1 19.0 %collective-permute-start.3 = (bf16[576,128]{1,0:T(8,128)(2,1)}, bf16[576,128]{1,0:T(8,128)(2,1)}, u32[]{:S(2)}, u32[]{:S(2)}) collective-permute-start(bf16[576,128]{1,0:T(8,128)(2,1)} %get-tuple-element.41), channel_id=1, source_target_pairs={{0,4},{4,0},{8,12},{12,8},{16,20},{20,16},{24,28},{28,24},{1,5},{5... | collective-permute-start | bytes 442376 | tf_op jit(solution)/shard_map/ppermute | solution.py:30
  6.0 15.5 %collective-permute-start.4 = (bf16[576,128]{1,0:T(8,128)(2,1)}, bf16[576,128]{1,0:T(8,128)(2,1)}, u32[]{:S(2)}, u32[]{:S(2)}) collective-permute-start(bf16[576,128]{1,0:T(8,128)(2,1)} %get-tuple-element.41), channel_id=1, source_target_pairs={{0,8},{4,12},{8,16},{12,20},{16,24},{20,28},{24,0},{28,4},{1,9},{5... | collective-permute-start | bytes 442376 | tf_op jit(solution)/shard_map/ppermute | solution.py:30
  11.5 31.7 %collective-permute-start = (bf16[1792,256]{1,0:T(8,128)(2,1)}, bf16[1792,256]{1,0:T(8,128)(2,1)}, u32[]{:S(2)}, u32[]{:S(2)}) collective-permute-start(bf16[1792,256]{1,0:T(8,128)(2,1)} %get-tuple-element.36), channel_id=1, source_target_pairs={{0,2},{1,3},{2,0},{3,1},{4,6},{5,7},{6,4},{7,5},{8,10},{9,11},{10,... | collective-permute-start | bytes 2752520 | tf_op jit(solution)/shard_map/ppermute | solution.py:30
  13.0 31.9 %collective-permute-start.1 = (bf16[1792,256]{1,0:T(8,128)(2,1)}, bf16[1792,256]{1,0:T(8,128)(2,1)}, u32[]{:S(2)}, u32[]{:S(2)}) collective-permute-start(bf16[1792,256]{1,0:T(8,128)(2,1)} %get-tuple-element.38), channel_id=1, source_target_pairs={{0,1},{1,0},{2,3},{3,2},{4,5},{5,4},{6,7},{7,6},{8,9},{9,8},{10,11... | collective-permute-start | bytes 2752520 | tf_op jit(solution)/shard_map/ppermute | solution.py:30
  13.0 40.8 %collective-permute-start.2 = (bf16[1792,256]{1,0:T(8,128)(2,1)}, bf16[1792,256]{1,0:T(8,128)(2,1)}, u32[]{:S(2)}, u32[]{:S(2)}) collective-permute-start(bf16[1792,256]{1,0:T(8,128)(2,1)} %get-tuple-element.35), channel_id=1, source_target_pairs={{0,3},{1,2},{2,1},{3,0},{4,7},{5,6},{6,5},{7,4},{8,11},{9,10},{10,... | collective-permute-start | bytes 2752520 | tf_op jit(solution)/shard_map/ppermute | solution.py:30
  13.8 4.0 %copy-start.4 = (bf16[128,2048]{1,0:T(8,128)(2,1)S(1)}, bf16[128,2048]{1,0:T(8,128)(2,1)}, u32[]{:S(2)}) copy-start(bf16[128,2048]{1,0:T(8,128)(2,1)} %param.15) | copy-start | bytes 1572868
  17.8 2.9 %copy-start.6 = (bf16[128,1024]{1,0:T(8,128)(2,1)S(1)}, bf16[128,1024]{1,0:T(8,128)(2,1)}, u32[]{:S(2)}) copy-start(bf16[128,1024]{1,0:T(8,128)(2,1)} %param.16) | copy-start | bytes 786436
  19.9 33.9 %copy-start.3 = (bf16[128,16,512]{0,2,1:T(8,128)(2,1)S(1)}, bf16[128,16,512]{0,2,1:T(8,128)(2,1)}, u32[]{:S(2)}) copy-start(bf16[128,16,512]{0,2,1:T(8,128)(2,1)} %convert_bitcast_fusion) | copy-start | bytes 6291460
  21.5 9.5 %collective-permute-start.5 = (bf16[576,128]{1,0:T(8,128)(2,1)}, bf16[576,128]{1,0:T(8,128)(2,1)S(1)}, u32[]{:S(2)}, u32[]{:S(2)}) collective-permute-start(bf16[576,128]{1,0:T(8,128)(2,1)} %collective-permute-done.4), channel_id=1, source_target_pairs={{0,4},{4,0},{8,12},{12,8},{16,20},{20,16},{24,28},{28,24},{1,5},{5... | collective-permute-start | bytes 442376 | tf_op jit(solution)/shard_map/ppermute | solution.py:30
  22.1 7.5 %collective-permute-start.6 = (bf16[576,128]{1,0:T(8,128)(2,1)}, bf16[576,128]{1,0:T(8,128)(2,1)S(1)}, u32[]{:S(2)}, u32[]{:S(2)}) collective-permute-start(bf16[576,128]{1,0:T(8,128)(2,1)} %collective-permute-done.4), channel_id=1, source_target_pairs={{0,8},{4,12},{8,16},{12,20},{16,24},{20,28},{24,0},{28,4},{1,9},{5... | collective-permute-start | bytes 442376 | tf_op jit(solution)/shard_map/ppermute | solution.py:30
  29.6 5.1 %collective-permute-start.7 = (bf16[576,128]{1,0:T(8,128)(2,1)S(1)}, bf16[576,128]{1,0:T(8,128)(2,1)S(1)}, u32[]{:S(2)}, u32[]{:S(2)}) collective-permute-start(bf16[576,128]{1,0:T(8,128)(2,1)S(1)} %collective-permute-done.6), channel_id=1, source_target_pairs={{0,4},{4,0},{8,12},{12,8},{16,20},{20,16},{24,28},{28,24},{1,5},{5... | collective-permute-start | bytes 442376 | tf_op jit(solution)/shard_map/ppermute | solution.py:30
  31.1 6.9 %collective-permute-start.8 = (bf16[576,128]{1,0:T(8,128)(2,1)S(1)}, bf16[576,128]{1,0:T(8,128)(2,1)S(1)}, u32[]{:S(2)}, u32[]{:S(2)}) collective-permute-start(bf16[576,128]{1,0:T(8,128)(2,1)S(1)} %collective-permute-done.6), channel_id=1, source_target_pairs={{0,8},{4,12},{8,16},{12,20},{16,24},{20,28},{24,0},{28,4},{1,9},{5... | collective-permute-start | bytes 442376 | tf_op jit(solution)/shard_map/ppermute | solution.py:30
  34.7 42.1 %collective-permute-start.10 = (bf16[1792,256]{1,0:T(8,128)(2,1)}, bf16[1792,256]{1,0:T(8,128)(2,1)}, u32[]{:S(2)}, u32[]{:S(2)}) collective-permute-start(bf16[1792,256]{1,0:T(8,128)(2,1)} %get-tuple-element.32), channel_id=1, source_target_pairs={{0,2},{1,3},{2,0},{3,1},{4,6},{5,7},{6,4},{7,5},{8,10},{9,11},{10,... | collective-permute-start | bytes 2752520 | tf_op jit(solution)/shard_map/ppermute | solution.py:30
  38.0 5.1 %collective-permute-start.9 = (bf16[576,128]{1,0:T(8,128)(2,1)S(1)}, bf16[576,128]{1,0:T(8,128)(2,1)S(1)}, u32[]{:S(2)}, u32[]{:S(2)}) collective-permute-start(bf16[576,128]{1,0:T(8,128)(2,1)S(1)} %collective-permute-done.8), channel_id=1, source_target_pairs={{0,4},{4,0},{8,12},{12,8},{16,20},{20,16},{24,28},{28,24},{1,5},{5... | collective-permute-start | bytes 442376 | tf_op jit(solution)/shard_map/ppermute | solution.py:30
  43.1 33.7 %collective-permute-start.11 = (bf16[1792,256]{1,0:T(8,128)(2,1)}, bf16[1792,256]{1,0:T(8,128)(2,1)}, u32[]{:S(2)}, u32[]{:S(2)}) collective-permute-start(bf16[1792,256]{1,0:T(8,128)(2,1)} %get-tuple-element.34), channel_id=1, source_target_pairs={{0,1},{1,0},{2,3},{3,2},{4,5},{5,4},{6,7},{7,6},{8,9},{9,8},{10,11... | collective-permute-start | bytes 2752520 | tf_op jit(solution)/shard_map/ppermute | solution.py:30
  43.2 48.1 %collective-permute-start.12 = (bf16[1792,256]{1,0:T(8,128)(2,1)}, bf16[1792,256]{1,0:T(8,128)(2,1)}, u32[]{:S(2)}, u32[]{:S(2)}) collective-permute-start(bf16[1792,256]{1,0:T(8,128)(2,1)} %get-tuple-element.31), channel_id=1, source_target_pairs={{0,3},{1,2},{2,1},{3,0},{4,7},{5,6},{6,5},{7,4},{8,11},{9,10},{10,... | collective-permute-start | bytes 2752520 | tf_op jit(solution)/shard_map/ppermute | solution.py:30
  53.8 5.6 %copy-start.7 = (bf16[128,1024]{0,1:T(8,128)(2,1)S(1)}, bf16[128,1024]{0,1:T(8,128)(2,1)}, u32[]{:S(2)}) copy-start(bf16[128,1024]{0,1:T(8,128)(2,1)} %copy.36) | copy-start | bytes 786436
  103.1 2.4 copy-start.2
  103.1 15.4 %copy-start.5 = (bf16[128,1792]{1,0:T(8,128)(2,1)S(1)}, bf16[128,1792]{1,0:T(8,128)(2,1)}, u32[]{:S(2)}) copy-start(bf16[128,1792]{1,0:T(8,128)(2,1)} %param.14) | copy-start | bytes 1376260
  103.2 2.3 collective-permute-start.14
  104.1 3.9 %collective-permute-start.13 = (bf16[128,1792]{1,0:T(8,128)(2,1)S(1)}, bf16[128,1792]{1,0:T(8,128)(2,1)S(1)}, u32[]{:S(2)}, u32[]{:S(2)}) collective-permute-start(bf16[128,1792]{1,0:T(8,128)(2,1)S(1)} %get-tuple-element.29), channel_id=1, source_target_pairs={{0,1},{1,0},{2,3},{3,2},{4,5},{5,4},{6,7},{7,6},{8,9},{9,8},{10,11... | collective-permute-start | bytes 1376264 | tf_op jit(solution)/shard_map/ppermute | solution.py:30
  105.6 12.9 %collective-permute-start.15 = (bf16[128,1792]{1,0:T(8,128)(2,1)S(1)}, bf16[128,1792]{1,0:T(8,128)(2,1)S(1)}, u32[]{:S(2)}, u32[]{:S(2)}) collective-permute-start(bf16[128,1792]{1,0:T(8,128)(2,1)S(1)} %add_convert_fusion.1), channel_id=1, source_target_pairs={{0,2},{1,3},{2,0},{3,1},{4,6},{5,7},{6,4},{7,5},{8,10},{9,11},{10,... | collective-permute-start | bytes 1376264 | tf_op jit(solution)/shard_map/ppermute | solution.py:30
  108.0 18.4 %copy-start.8 = (s32[128,4]{0,1:T(4,128)S(1)}, s32[128,4]{0,1:T(4,128)}, u32[]{:S(2)}) copy-start(s32[128,4]{0,1:T(4,128)} %param.24) | copy-start | bytes 6148
  121.3 1.3 collective-permute-start.16
  122.6 3.7 %collective-permute-start.17 = (f32[9,128]{1,0:T(8,128)S(1)}, f32[9,128]{1,0:T(8,128)S(1)}, u32[]{:S(2)}, u32[]{:S(2)}) collective-permute-start(f32[9,128]{1,0:T(8,128)S(1)} %fusion.36), channel_id=1, source_target_pairs={{0,2},{1,3},{2,0},{3,1},{4,6},{5,7},{6,4},{7,5},{8,10},{9,11},{10,... | collective-permute-start | bytes 13832 | tf_op jit(solution)/shard_map/ppermute | solution.py:30
  127.6 118.7 %copy-start.1 = (bf16[16,128,512]{2,1,0:T(8,128)(2,1)S(1)}, bf16[16,128,512]{2,1,0:T(8,128)(2,1)}, u32[]{:S(2)}) copy-start(bf16[16,128,512]{2,1,0:T(8,128)(2,1)} %param.19) | copy-start | bytes 6291460

commit v3 on v2

--- a/solution.py
+++ b/solution.py
@@ -79,16 +79,25 @@
             column.append(over_ctx(column[-1], 1, 0))
         return [[b] + [over_ctx(b, 0, dx) for dx in range(1, nx)] for b in column]
 
+    offsets = [(dy, dc) for dc in range(nc) for dy in range(ny)]
+
+    def pieces(weight, dim):
+        return [
+            lax.dynamic_slice_in_dim(weight[0], tp_at(dy, dc) * col_width, col_width, dim)
+            for dy, dc in offsets
+        ]
+
+    def exchange(cut):
+        return [over_tp(p, *at) if at != (0, 0) else p for p, at in zip(cut, offsets)]
+
+    latent_kv, *gate_cut = lax.optimization_barrier((latent_kv, *pieces(gate_proj, 0)))
+    gates = exchange(gate_cut)
+    ups = exchange(pieces(up_proj, 0))
+    near = [i for i, (dy, dc) in enumerate(offsets) if not (dy and dc)]
+    down_cut = [pieces(down_proj, 1)[i] for i in near]
+
     keys = jnp.concatenate([latent_kv, key_rope], axis=0)
     key_blocks = gather_ctx(keys)
-
-    def exchanged(weight, dy, dc):
-        piece = lax.dynamic_slice_in_dim(weight[0], tp_at(dy, dc) * col_width, col_width, 0)
-        return over_tp(piece, dy, dc) if (dy or dc) else piece
-
-    offsets = [(dy, dc) for dc in range(nc) for dy in range(ny)]
-    gates = [exchanged(gate_proj, dy, dc) for dy, dc in offsets]
-    ups = [exchanged(up_proj, dy, dc) for dy, dc in offsets]
 
     query_pos = ctx * row_count + jnp.arange(row_count, dtype=jnp.int32)
     query_lat = jnp.einsum(
@@ -124,12 +133,16 @@
     heads_out = jnp.einsum(
         "thl,hlv->thv", attn_lat, absorb_value, preferred_element_type=jnp.float32
     ).astype(jnp.bfloat16)
-    heads_out, *ups = lax.optimization_barrier((heads_out, *ups))
+    heads_out, *rest = lax.optimization_barrier((heads_out, *ups[:-1], *down_cut))
+    ups[:-1], down_cut = rest[: len(ups) - 1], rest[len(ups) - 1 :]
+    downs = [over_tp(p, *offsets[i]) if i else p for p, i in zip(down_cut, near)]
     attn_part = jnp.dot(
         heads_out.reshape(row_count, head_count * VDIM),
         out_proj,
         preferred_element_type=jnp.float32,
     )
+
+    attn_part, ups[-1] = lax.optimization_barrier((attn_part, ups[-1]))
 
     def own_part(dy, dc):
         return lax.dynamic_slice_in_dim(attn_part, tp_at(dy, dc) * col_width, col_width, 1)
@@ -172,7 +185,7 @@
     low = (dense_gates.T - high.astype(jnp.float32)).astype(jnp.bfloat16)
     fill = jnp.zeros((row_count, META // 2 - expert_count), jnp.bfloat16)
     packet = jnp.concatenate([tokens, high, fill, low, fill], axis=1)
-    routed_sum = expert_call((nz, nx, ny, nc), packet, gates, ups, down_proj[0])
+    routed_sum = expert_call((nz, nx, ny, nc), packet, gates, ups, downs, down_proj[0])
     return (residual + routed_sum).astype(jnp.bfloat16)
 
 
@@ -181,10 +194,16 @@
     n_tp = ny * nc
     packet, refs = refs[0], refs[1:]
     gates, ups, refs = refs[:n_tp], refs[n_tp : 2 * n_tp], refs[2 * n_tp :]
-    down, out = refs[0], refs[1]
-    (tok, dmat, own, core_out, core_in, y_out, y_in, hid, acc, x_out, x_in, z_out, z_in) = refs[2:15]
-    (s_z, r_z, s_x, r_x, s_d, r_d, s_c, r_c, s_y, r_y) = refs[15:25]
-    (s_hy, r_hy, s_hc, r_hc, s_bx, r_bx, s_bz, r_bz, local_sem) = refs[25:]
+    offsets = [(dy, dc) for dc in range(nc) for dy in range(ny)]
+    near = [at for at in offsets if not (at[0] and at[1])]
+    far = [at for at in offsets if at[0] and at[1]]
+    downs, refs = dict(zip(near, refs[: len(near)])), refs[len(near) :]
+    down, out, dmat = refs[:3]
+    refs = refs[3:]
+    (tok, own, core_out, core_in, y_out, y_in, hid, acc, x_out, x_in, z_out, z_in) = refs[:12]
+    (s_z, r_z, s_x, r_x, s_c, r_c, s_y, r_y) = refs[12:20]
+    s_d, r_d = refs[28:]
+    (s_hy, r_hy, s_hc, r_hc, s_bx, r_bx, s_bz, r_bz) = refs[20:28]
     rows, width = out.shape
     h = down.shape[0]
     ctx, tp = lax.axis_index("ctx"), lax.axis_index("tp")
@@ -213,7 +232,7 @@
         peers.append(ctx_at(1, 0))
     if nz > 2:
         peers.append(ctx_at(-1, 0))
-    peers += [tp_at(dy, dc) for dc in range(nc) for dy in range(ny) if dy or dc]
+    peers += [tp_at(*at) for at in offsets[1:]]
     barrier = pltpu.get_barrier_semaphore()
     for peer in peers:
         pl.semaphore_signal(
@@ -222,7 +241,7 @@
     pl.semaphore_wait(barrier, len(peers))
 
     sent = []
-    zc, xc, dcp, cc, yc, hyc, hcc, bxc, bzc = ({} for _ in range(9))
+    zc, xc, cc, yc, hyc, hcc, bxc, bzc = ({} for _ in range(8))
 
     def pass_on(dz):
         block = packet if dz == 0 else tok.at[dz, pl.ds(0, rows)]
@@ -243,25 +262,7 @@
             )
             sent.append(xc[dz, dx])
 
-    def down_cols(dy, dc):
-        begin = tp_at(dy, dc)[1] * width
-        return down.at[:, pl.ds(pl.multiple_of(begin, 128), width)]
-
     pass_on(0)
-    mine = pltpu.make_async_copy(down_cols(0, 0), dmat.at[pl.ds(0, h)], local_sem)
-    mine.start()
-    for dc in range(nc - 1, -1, -1):
-        for dy in range(ny):
-            if dy or dc:
-                k = dc * ny + dy
-                dcp[k] = push(
-                    down_cols(dy, dc),
-                    dmat.at[pl.ds(k * h, h)],
-                    s_d.at[k - 1],
-                    r_d.at[k - 1],
-                    tp_at(dy, dc),
-                )
-                sent.append(dcp[k])
     tok[0, pl.ds(0, rows), :] = packet[...]
 
     def products(dz):
@@ -311,6 +312,17 @@
             else:
                 own[dz, 0] = value
 
+    far_copies = []
+
+    def send_down():
+        for i, at in enumerate(far):
+            begin = pl.multiple_of(tp_at(*at)[1] * width, 128)
+            downs[at] = dmat.at[i]
+            far_copies.append(
+                push(down.at[:, pl.ds(begin, width)], dmat.at[i], s_d.at[i], r_d.at[i], tp_at(*at))
+            )
+            sent.append(far_copies[-1])
+
     def activate(dz):
         value = own[dz, 0]
         for dy in range(1, ny):
@@ -343,22 +355,26 @@
 
     step = 256 if width % 256 == 0 else 128
 
-    def outputs(dz, first):
+    def outputs(dz):
+        if dz == 0:
+            for copy in far_copies:
+                copy.wait_recv()
         for dc in range(1, nc):
             hcc[dz, dc].wait_recv()
-        if first:
-            mine.wait()
-            for k in dcp:
-                dcp[k].wait_recv()
         meta = tok[dz, :, pl.ds(width, META)].astype(jnp.float32)
         lane = lax.broadcasted_iota(jnp.int32, meta.shape, 1)
         picked = (lane == ctx) | (lane == ctx + META // 2)
         gate = jnp.sum(jnp.where(picked, meta, 0.0), axis=1, keepdims=True)
         for j in range(width // step):
             cols = pl.ds(j * step, step)
-            value = gate * jnp.dot(
-                hid[dz], dmat[:, cols], preferred_element_type=jnp.float32
-            )
+            value = jnp.zeros((nx * rows, step), jnp.float32)
+            for k, at in enumerate(offsets):
+                value = value + jnp.dot(
+                    hid[dz, :, pl.ds(k * h, h)],
+                    downs[at][:, cols],
+                    preferred_element_type=jnp.float32,
+                )
+            value = value * gate
             acc[dz, :, cols] = value[:rows]
             for dx in range(1, nx):
                 x_out[dz, dx - 1, :, cols] = value[dx * rows : (dx + 1) * rows].astype(jnp.bfloat16)
@@ -397,12 +413,14 @@
             products(turn)
         if 0 <= turn - 1 < nz:
             chip_sums(turn - 1)
+        if turn == 1:
+            send_down()
         if 0 <= turn - 2 < nz:
             share_hidden(turn - 2)
         if 0 <= turn - 1 < nz:
             activate(turn - 1)
         if 0 <= turn - 2 < nz:
-            outputs(turn - 2, turn == 2)
+            outputs(turn - 2)
         if 1 <= turn - 3 < nz:
             give_back(turn - 3)
     give_back(0)
@@ -410,20 +428,21 @@
         copy.wait_send()
 
 
-def expert_call(dims, packet, gates, ups, down):
+def expert_call(dims, packet, gates, ups, downs, down):
     nz, nx, ny, nc = dims
     n_tp = ny * nc
     rows = packet.shape[0]
     width = packet.shape[1] - META
     h = down.shape[0]
+    n_far = max(n_tp - len(downs), 1)
     all_rows = nx * rows
     px, py, pc, pz = max(nx - 1, 1), max(ny - 1, 1), max(nc - 1, 1), max(nz - 1, 1)
     bf16, f32 = jnp.bfloat16, jnp.float32
     vmem = pl.BlockSpec(memory_space=pltpu.VMEM)
     sem = pltpu.SemaphoreType.DMA
     shapes = [
+        pltpu.VMEM((n_far, h, width), bf16),
         pltpu.VMEM((nz, all_rows, width + META), bf16),
-        pltpu.VMEM((n_tp * h, width), bf16),
         pltpu.VMEM((nz, ny, all_rows, 2 * h), f32),
         pltpu.VMEM((nz, pc, all_rows, ny * 2 * h), bf16),
         pltpu.VMEM((nz, pc, all_rows, ny * 2 * h), bf16),
@@ -437,15 +456,15 @@
         pltpu.VMEM((pz, rows, width), bf16),
     ]
     sems = []
-    for shape in ((pz,), (nz, px), (n_tp,), (nz, pc), (nz, py), (nz, py), (nz, pc), (nz, px), (pz,)):
+    for shape in ((pz,), (nz, px), (nz, pc), (nz, py), (nz, py), (nz, pc), (nz, px), (pz,), (n_far,)):
         sems += [sem(shape), sem(shape)]
     flops = 2 * nz * all_rows * width * n_tp * h * 3
     return pl.pallas_call(
         functools.partial(expert_kernel, dims),
         out_shape=jax.ShapeDtypeStruct((rows, width), f32),
-        in_specs=[vmem] * (1 + 2 * n_tp) + [pl.BlockSpec(memory_space=pl.ANY)],
+        in_specs=[vmem] * (1 + 2 * n_tp + len(downs)) + [pl.BlockSpec(memory_space=pl.ANY)],
         out_specs=vmem,
-        scratch_shapes=shapes + sems + [sem],
+        scratch_shapes=shapes + sems,
         compiler_params=pltpu.CompilerParams(
             collective_id=1, has_side_effects=True, vmem_limit_bytes=58 * 1024 * 1024
         ),
@@ -453,7 +472,7 @@
             flops=flops, bytes_accessed=16 * 1024 * 1024, transcendentals=0
         ),
         name="experts",
-    )(packet, *gates, *ups, down)
+    )(packet, *gates, *ups, *downs, down)
 
 
 def solution(mesh):

time: 247 us -> 257 us (1.040)
  waiting for transfers between devices: 52.4 us -> 57.5 us
  Pallas kernels: 117 us -> 122 us
    ppermute x18 -> x20, waiting for transfers between devices: 52.4 us -> 57.5 us  [move(): return lax.ppermute(value, axis, pairs)]
    pallas_call x1, Pallas kernels: 117 us -> 122 us  [expert_call(): pl.pallas_call(functools.partial(expert_kernel, dims), out_shape=jax.Shap...]
    dynamic_slice x2 -> x3, local copies, waits for them, and re-layouts: 7.85 us -> 9.66 us  [pieces(): lax.dynamic_slice_in_dim(weight[0], tp_at(dy, dc) * col_width, col_width,...]
    ppermute x18 -> x20, starting transfers between devices: 18.2 us -> 18.7 us  [move(): return lax.ppermute(value, axis, pairs)]
  transfers between devices with their start and end apart: 18 -> 20, of which waited for: 10 -> 11; matrix products, arithmetic and copies ran while one was open for 15% -> 19% of each run, Pallas kernels for 0% -> 0%
where the time goes in v3:
time: 257 us
  Pallas kernels  122 us (47%)
  waiting for transfers between devices  57.5 us (22%)
  matrix products  37.9 us (15%)
  starting transfers between devices  18.7 us (7%)
  local copies, waits for them, and re-layouts  15.5 us (6%)
  other arithmetic  5.65 us (2%)
    pallas_call x1, Pallas kernels, expert_call(): pl.pallas_call(functools.partial(expert_kernel, dims), out_shape=jax.Shap...  122 us
    ppermute x20, waiting for transfers between devices, move(): return lax.ppermute(value, axis, pairs)  57.5 us
    ppermute x20, starting transfers between devices, move(): return lax.ppermute(value, axis, pairs)  18.7 us
    sub x1, matrix products, body(): scores - top_score[:, :, None]  11.6 us
    dot_general x1, matrix products, body(): jnp.dot(heads_out.reshape(row_count, head_count * VDIM), out_proj, prefer...  11.5 us
    dynamic_slice x3, local copies, waits for them, and re-layouts, pieces(): lax.dynamic_slice_in_dim(weight[0], tp_at(dy, dc) * col_width, col_width,...  9.66 us
    dot_general x1, matrix products, body(): jnp.einsum('thl,hlv->thv', attn_lat, absorb_value, preferred_element_type...  5.8 us
    dot_general x1, matrix products, body(): jnp.einsum('thl,ls->ths', query_lat, latent, preferred_element_type=jnp.f...  5.63 us
  transfers between devices with their start and end apart: 20, of which 11 were waited for; matrix products, arithmetic and copies ran while one was open for 19% of the time, Pallas kernels for 0%

profile of v3, /device:TPU:0, one launch (start us, length us, event | category | flops | bytes accessed | tf_op | source)
XLA Modules:
  0.0 257.1 jit_solution(12331765712588144195)
XLA Ops:
  0.0 4.0 %dynamic-slice_bitcast_fusion.7 = (bf16[1792,256]{1,0:T(8,128)(2,1)}, bf16[1792,256]{1,0:T(8,128)(2,1)}, bf16[1792,256]{1,0:T(8,128)(2,1)}, bf16[1792,256]{1,0:T(8,128)(2,1)}) fusion(bf16[1,7168,256]{2,1,0:T(8,128)(2,1)} %param.25, s32[]{:T(128)S(6)} %select_n.189, s32[]{:T(128)S(6)} %select_n.186, s32[]{:T(128)S(6)} %select_n.184, s32[]{:T(128)S(6)} %select_n.188), kind=kLoop, calls=%fused_computation.31 | loop fusion | bytes 7340048 | tf_op jit(solution)/shard_map/dynamic_slice | solution.py:86
  4.0 0.7 constant_dynamic-update-slice_fusion.1
  4.7 0.6 constant_dynamic-update-slice_fusion
  5.3 3.0 %collective-permute-start.3 = (bf16[576,128]{1,0:T(8,128)(2,1)}, bf16[576,128]{1,0:T(8,128)(2,1)}, u32[]{:S(2)}, u32[]{:S(2)}) collective-permute-start(bf16[576,128]{1,0:T(8,128)(2,1)} %get-tuple-element.62), channel_id=1, source_target_pairs={{0,4},{4,0},{8,12},{12,8},{16,20},{20,16},{24,28},{28,24},{1,5},{5... | collective-permute-start | bytes 442376 | tf_op jit(solution)/shard_map/ppermute | solution.py:30
  8.3 1.6 collective-permute-start.4
  9.8 1.5 collective-permute-start
  11.4 0.6 collective-permute-start.2
  12.2 4.1 %dynamic-slice_bitcast_fusion = (bf16[1792,256]{1,0:T(8,128)(2,1)}, bf16[1792,256]{1,0:T(8,128)(2,1)}, bf16[1792,256]{1,0:T(8,128)(2,1)}, bf16[1792,256]{1,0:T(8,128)(2,1)}) fusion(bf16[1,7168,256]{2,1,0:T(8,128)(2,1)} %param.26, s32[]{:T(128)S(6)} %select_n.189, s32[]{:T(128)S(6)} %select_n.186, s32[]{:T(128)S(6)} %select_n.184, s32[]{:T(128)S(6)} %select_n.188), kind=kLoop, calls=%fused_computation.24 | loop fusion | bytes 7340048 | tf_op jit(solution)/shard_map/dynamic_slice | solution.py:86
  16.2 1.6 dynamic-slice_bitcast_fusion.1
  17.8 2.1 convert_bitcast_fusion
  19.9 0.8 broadcast_compare_fusion
  20.7 0.8 copy.36
  21.6 0.5 collective-permute-start.5
  22.1 1.6 collective-permute-start.6
  23.7 1.0 constant_dynamic-update-slice_fusion.8
  24.7 1.0 constant_dynamic-update-slice_fusion.7
  25.6 4.0 %collective-permute-done.6 = bf16[576,128]{1,0:T(8,128)(2,1)S(1)} collective-permute-done((bf16[576,128]{1,0:T(8,128)(2,1)}, bf16[576,128]{1,0:T(8,128)(2,1)S(1)}, u32[]{:S(2)}, u32[]{:S(2)}) %collective-permute-start.6) | collective-permute-done | bytes 147488 | tf_op jit(solution)/shard_map/ppermute | solution.py:30
  29.6 1.5 collective-permute-start.7
  31.2 3.5 %collective-permute-done.7 = bf16[576,128]{1,0:T(8,128)(2,1)S(1)} collective-permute-done((bf16[576,128]{1,0:T(8,128)(2,1)S(1)}, bf16[576,128]{1,0:T(8,128)(2,1)S(1)}, u32[]{:S(2)}, u32[]{:S(2)}) %collective-permute-start.7) | collective-permute-done | bytes 147488 | tf_op jit(solution)/shard_map/ppermute | solution.py:30
  34.7 1.5 collective-permute-start.10
  36.3 1.8 collective-permute-done.8
  38.0 0.5 collective-permute-start.9
  38.7 4.5 %collective-permute-done.9 = bf16[576,128]{1,0:T(8,128)(2,1)S(1)} collective-permute-done((bf16[576,128]{1,0:T(8,128)(2,1)S(1)}, bf16[576,128]{1,0:T(8,128)(2,1)S(1)}, u32[]{:S(2)}, u32[]{:S(2)}) %collective-permute-start.9) | collective-permute-done | bytes 147488 | tf_op jit(solution)/shard_map/ppermute | solution.py:30
  43.3 1.7 collective-permute-start.12
  45.0 7.2 %collective-permute-done.2.refs_4_ = bf16[1792,256]{1,0:T(8,128)(2,1)} collective-permute-done((bf16[1792,256]{1,0:T(8,128)(2,1)}, bf16[1792,256]{1,0:T(8,128)(2,1)}, u32[]{:S(2)}, u32[]{:S(2)}) %collective-permute-start.2) | collective-permute-done | bytes 917536 | tf_op jit(solution)/shard_map/ppermute | solution.py:30
  52.2 5.6 %fusion.25 = f32[128,16,1024]{2,0,1:T(8,128)} fusion(bf16[128,16,512]{0,2,1:T(8,128)(2,1)S(1)} %copy-done.3, bf16[576,1024]{1,0:T(8,128)(2,1)S(1)} %constant_dynamic-update-slice_fusion.2), kind=kOutput, calls=%fused_computation.37 | convolution fusion | flops 2147483648 | bytes 11534336 | tf_op jit(solution)/shard_map/thl,ls->ths/dot_general | solution.py:121
  57.8 11.6 %fusion.40 = (f32[128,16]{0,1:T(8,128)S(1)}, bf16[128,16,1024]{2,0,1:T(8,128)(2,1)}) fusion(pred[128,1024]{1,0:T(8,128)(4,1)} %broadcast_compare_fusion, f32[128,16,1024]{2,0,1:T(8,128)} %fusion.25, bf16[128,16,64]{0,2,1:T(8,128)(2,1)S(1)} %bitcast.97, bf16[576,1024]{1,0:T(8,128)(2,1)S(1)} %constant_dynamic-update-slice_fusion.2), kind=kOutput, calls=%fused_computation.79 | convolution fusion | flops 555746304 | bytes 22028288 | tf_op jit(solution)/shard_map/sub | solution.py:127
  69.4 5.8 %fusion.18 = bf16[128,16,128]{2,0,1:T(8,128)(2,1)S(1)} fusion(bf16[16,512,128]{2,1,0:T(8,128)(2,1)} %param.20, f32[128,16]{0,1:T(8,128)S(1)} %get-tuple-element.64, bf16[128,16,1024]{2,0,1:T(8,128)(2,1)} %get-tuple-element.65, bf16[576,1024]{1,0:T(8,128)(2,1)S(1)} %constant_dynamic-update-slice_fusion.2), kind=kOutput, calls=%fused_computation.14 | convolution fusion | flops 2418278400 | bytes 7872512 | tf_op jit(solution)/shard_map/thl,hlv->thv/dot_general | solution.py:133
  75.2 0.3 copy.38
  75.5 11.5 %fusion.41 = f32[128,7168]{1,0:T(8,128)S(1)} fusion(bf16[128,2048]{0,1:T(8,128)(2,1)S(1)} %bitcast.95, bf16[2048,7168]{1,0:T(8,128)(2,1)} %param.21), kind=kOutput, calls=%fused_computation.80 | convolution fusion | flops 3758096384 | bytes 33554432 | tf_op jit(solution)/shard_map/dot_general | solution.py:139
  87.0 2.7 %collective-permute-done.12.refs_8_ = bf16[1792,256]{1,0:T(8,128)(2,1)} collective-permute-done((bf16[1792,256]{1,0:T(8,128)(2,1)}, bf16[1792,256]{1,0:T(8,128)(2,1)}, u32[]{:S(2)}, u32[]{:S(2)}) %collective-permute-start.12) | collective-permute-done | bytes 917536 | tf_op jit(solution)/shard_map/ppermute | solution.py:30
  89.8 0.8 collective-permute-start.14
  90.7 1.4 collective-permute-done.14
  92.2 1.6 collective-permute-start.15
  93.8 0.8 dynamic-slice_convert_fusion.2
  94.6 10.6 %collective-permute-done.15 = bf16[128,1792]{1,0:T(8,128)(2,1)} collective-permute-done((bf16[128,1792]{1,0:T(8,128)(2,1)S(1)}, bf16[128,1792]{1,0:T(8,128)(2,1)}, u32[]{:S(2)}, u32[]{:S(2)}) %collective-permute-start.15) | collective-permute-done | bytes 458784 | tf_op jit(solution)/shard_map/ppermute | solution.py:30
  105.2 1.6 multiply_reduce_fusion
  106.8 1.3 fusion.23
  108.2 1.2 collective-permute-done.16
  109.4 1.6 collective-permute-start.17
  110.9 0.5 collective-permute-start.18
  111.4 1.6 collective-permute-done.17
  113.1 0.1 copy.39
  113.3 0.1 multiply_convert_fusion
  113.4 0.9 concatenate.19.refs_0_
  114.4 19.0 %collective-permute-done.18.refs_10_ = bf16[256,1792]{1,0:T(8,128)(2,1)} collective-permute-done((bf16[256,1792]{1,0:T(8,128)(2,1)}, bf16[256,1792]{1,0:T(8,128)(2,1)}, u32[]{:S(2)}, u32[]{:S(2)}) %collective-permute-start.18) | collective-permute-done | bytes 917536 | tf_op jit(solution)/shard_map/ppermute | solution.py:30
  133.4 121.6 %experts.1 = f32[128,1792]{1,0:T(8,128)} custom-call(bf16[128,1920]{1,0:T(8,128)(2,1)} %concatenate.19.refs_0_, bf16[1792,256]{1,0:T(8,128)(2,1)} %get-tuple-element.32.refs_1_, bf16[1792,256]{1,0:T(8,128)(2,1)} %collective-permute-done.refs_2_, bf16[1792,256]{1,0:T(8,128)(2,1)} %collective-permute-done.1.refs_3_, ...), custom_call_target="tpu_custom_call" | custom-call | flops 11274289152 | bytes 16777216 | tf_op jit(solution)/shard_map/experts/pallas_call | solution.py:462
  255.0 2.0 add_convert_fusion
  (63 shorter events, 1.0 us)
Async XLA Ops:
  0.0 17.8 %copy-start = (bf16[16,128,512]{2,1,0:T(8,128)(2,1)S(1)}, bf16[16,128,512]{2,1,0:T(8,128)(2,1)}, u32[]{:S(2)}) copy-start(bf16[16,128,512]{2,1,0:T(8,128)(2,1)} %param.19) | copy-start | bytes 6291460
  0.0 4.0 %copy-start.10 = (bf16[512,128]{1,0:T(8,128)(2,1)S(1)}, bf16[512,128]{1,0:T(8,128)(2,1)}, u32[]{:S(2)}) copy-start(bf16[512,128]{1,0:T(8,128)(2,1)} %param.17) | copy-start | bytes 393220
  0.0 4.7 %copy-start.11 = (bf16[64,128]{1,0:T(8,128)(2,1)S(1)}, bf16[64,128]{1,0:T(8,128)(2,1)}, u32[]{:S(2)}) copy-start(bf16[64,128]{1,0:T(8,128)(2,1)} %param.18) | copy-start | bytes 49156
  5.3 16.8 %collective-permute-start.3 = (bf16[576,128]{1,0:T(8,128)(2,1)}, bf16[576,128]{1,0:T(8,128)(2,1)}, u32[]{:S(2)}, u32[]{:S(2)}) collective-permute-start(bf16[576,128]{1,0:T(8,128)(2,1)} %get-tuple-element.62), channel_id=1, source_target_pairs={{0,4},{4,0},{8,12},{12,8},{16,20},{20,16},{24,28},{28,24},{1,5},{5... | collective-permute-start | bytes 442376 | tf_op jit(solution)/shard_map/ppermute | solution.py:30
  8.3 13.3 %collective-permute-start.4 = (bf16[576,128]{1,0:T(8,128)(2,1)}, bf16[576,128]{1,0:T(8,128)(2,1)}, u32[]{:S(2)}, u32[]{:S(2)}) collective-permute-start(bf16[576,128]{1,0:T(8,128)(2,1)} %get-tuple-element.62), channel_id=1, source_target_pairs={{0,8},{4,12},{8,16},{12,20},{16,24},{20,28},{24,0},{28,4},{1,9},{5... | collective-permute-start | bytes 442376 | tf_op jit(solution)/shard_map/ppermute | solution.py:30
  9.8 33.4 %collective-permute-start = (bf16[1792,256]{1,0:T(8,128)(2,1)}, bf16[1792,256]{1,0:T(8,128)(2,1)}, u32[]{:S(2)}, u32[]{:S(2)}) collective-permute-start(bf16[1792,256]{1,0:T(8,128)(2,1)} %get-tuple-element.25), channel_id=1, source_target_pairs={{0,2},{1,3},{2,0},{3,1},{4,6},{5,7},{6,4},{7,5},{8,10},{9,11},{10,... | collective-permute-start | bytes 2752520 | tf_op jit(solution)/shard_map/ppermute | solution.py:30
  11.4 33.6 %collective-permute-start.1 = (bf16[1792,256]{1,0:T(8,128)(2,1)}, bf16[1792,256]{1,0:T(8,128)(2,1)}, u32[]{:S(2)}, u32[]{:S(2)}) collective-permute-start(bf16[1792,256]{1,0:T(8,128)(2,1)} %get-tuple-element.26), channel_id=1, source_target_pairs={{0,1},{1,0},{2,3},{3,2},{4,5},{5,4},{6,7},{7,6},{8,9},{9,8},{10,11... | collective-permute-start | bytes 2752520 | tf_op jit(solution)/shard_map/ppermute | solution.py:30
  11.4 40.8 %collective-permute-start.2 = (bf16[1792,256]{1,0:T(8,128)(2,1)}, bf16[1792,256]{1,0:T(8,128)(2,1)}, u32[]{:S(2)}, u32[]{:S(2)}) collective-permute-start(bf16[1792,256]{1,0:T(8,128)(2,1)} %get-tuple-element.27), channel_id=1, source_target_pairs={{0,3},{1,2},{2,1},{3,0},{4,7},{5,6},{6,5},{7,4},{8,11},{9,10},{10,... | collective-permute-start | bytes 2752520 | tf_op jit(solution)/shard_map/ppermute | solution.py:30
  12.2 4.1 %copy-start.4 = (bf16[1,256,7168]{2,1,0:T(8,128)(2,1)S(1)}, bf16[1,256,7168]{2,1,0:T(8,128)(2,1)}, u32[]{:S(2)}) copy-start(bf16[1,256,7168]{2,1,0:T(8,128)(2,1)} %param.27) | copy-start | bytes 11010052
  16.2 1.6 copy-start.6
  17.8 2.9 %copy-start.8 = (bf16[128,1024]{1,0:T(8,128)(2,1)S(1)}, bf16[128,1024]{1,0:T(8,128)(2,1)}, u32[]{:S(2)}) copy-start(bf16[128,1024]{1,0:T(8,128)(2,1)} %param.16) | copy-start | bytes 786436
  19.9 32.2 %copy-start.3 = (bf16[128,16,512]{0,2,1:T(8,128)(2,1)S(1)}, bf16[128,16,512]{0,2,1:T(8,128)(2,1)}, u32[]{:S(2)}) copy-start(bf16[128,16,512]{0,2,1:T(8,128)(2,1)} %convert_bitcast_fusion) | copy-start | bytes 6291460
  21.6 9.5 %collective-permute-start.5 = (bf16[576,128]{1,0:T(8,128)(2,1)}, bf16[576,128]{1,0:T(8,128)(2,1)S(1)}, u32[]{:S(2)}, u32[]{:S(2)}) collective-permute-start(bf16[576,128]{1,0:T(8,128)(2,1)} %collective-permute-done.4), channel_id=1, source_target_pairs={{0,4},{4,0},{8,12},{12,8},{16,20},{20,16},{24,28},{28,24},{1,5},{5... | collective-permute-start | bytes 442376 | tf_op jit(solution)/shard_map/ppermute | solution.py:30
  22.1 7.5 %collective-permute-start.6 = (bf16[576,128]{1,0:T(8,128)(2,1)}, bf16[576,128]{1,0:T(8,128)(2,1)S(1)}, u32[]{:S(2)}, u32[]{:S(2)}) collective-permute-start(bf16[576,128]{1,0:T(8,128)(2,1)} %collective-permute-done.4), channel_id=1, source_target_pairs={{0,8},{4,12},{8,16},{12,20},{16,24},{20,28},{24,0},{28,4},{1,9},{5... | collective-permute-start | bytes 442376 | tf_op jit(solution)/shard_map/ppermute | solution.py:30
  29.6 5.1 %collective-permute-start.7 = (bf16[576,128]{1,0:T(8,128)(2,1)S(1)}, bf16[576,128]{1,0:T(8,128)(2,1)S(1)}, u32[]{:S(2)}, u32[]{:S(2)}) collective-permute-start(bf16[576,128]{1,0:T(8,128)(2,1)S(1)} %collective-permute-done.6), channel_id=1, source_target_pairs={{0,4},{4,0},{8,12},{12,8},{16,20},{20,16},{24,28},{28,24},{1,5},{5... | collective-permute-start | bytes 442376 | tf_op jit(solution)/shard_map/ppermute | solution.py:30
  31.1 6.9 %collective-permute-start.8 = (bf16[576,128]{1,0:T(8,128)(2,1)S(1)}, bf16[576,128]{1,0:T(8,128)(2,1)S(1)}, u32[]{:S(2)}, u32[]{:S(2)}) collective-permute-start(bf16[576,128]{1,0:T(8,128)(2,1)S(1)} %collective-permute-done.6), channel_id=1, source_target_pairs={{0,8},{4,12},{8,16},{12,20},{16,24},{20,28},{24,0},{28,4},{1,9},{5... | collective-permute-start | bytes 442376 | tf_op jit(solution)/shard_map/ppermute | solution.py:30
  34.7 40.5 %collective-permute-start.10 = (bf16[1792,256]{1,0:T(8,128)(2,1)}, bf16[1792,256]{1,0:T(8,128)(2,1)}, u32[]{:S(2)}, u32[]{:S(2)}) collective-permute-start(bf16[1792,256]{1,0:T(8,128)(2,1)} %get-tuple-element.50), channel_id=1, source_target_pairs={{0,2},{1,3},{2,0},{3,1},{4,6},{5,7},{6,4},{7,5},{8,10},{9,11},{10,... | collective-permute-start | bytes 2752520 | tf_op jit(solution)/shard_map/ppermute | solution.py:30
  38.0 5.1 %collective-permute-start.9 = (bf16[576,128]{1,0:T(8,128)(2,1)S(1)}, bf16[576,128]{1,0:T(8,128)(2,1)S(1)}, u32[]{:S(2)}, u32[]{:S(2)}) collective-permute-start(bf16[576,128]{1,0:T(8,128)(2,1)S(1)} %collective-permute-done.8), channel_id=1, source_target_pairs={{0,4},{4,0},{8,12},{12,8},{16,20},{20,16},{24,28},{28,24},{1,5},{5... | collective-permute-start | bytes 442376 | tf_op jit(solution)/shard_map/ppermute | solution.py:30
  43.2 32.0 %collective-permute-start.11 = (bf16[1792,256]{1,0:T(8,128)(2,1)}, bf16[1792,256]{1,0:T(8,128)(2,1)}, u32[]{:S(2)}, u32[]{:S(2)}) collective-permute-start(bf16[1792,256]{1,0:T(8,128)(2,1)} %get-tuple-element.52), channel_id=1, source_target_pairs={{0,1},{1,0},{2,3},{3,2},{4,5},{5,4},{6,7},{7,6},{8,9},{9,8},{10,11... | collective-permute-start | bytes 2752520 | tf_op jit(solution)/shard_map/ppermute | solution.py:30
  43.2 14.5 %copy-start.9 = (bf16[128,1024]{0,1:T(8,128)(2,1)S(1)}, bf16[128,1024]{0,1:T(8,128)(2,1)}, u32[]{:S(2)}) copy-start(bf16[128,1024]{0,1:T(8,128)(2,1)} %copy.36) | copy-start | bytes 786436
  43.3 46.5 %collective-permute-start.12 = (bf16[1792,256]{1,0:T(8,128)(2,1)}, bf16[1792,256]{1,0:T(8,128)(2,1)}, u32[]{:S(2)}, u32[]{:S(2)}) collective-permute-start(bf16[1792,256]{1,0:T(8,128)(2,1)} %get-tuple-element.49), channel_id=1, source_target_pairs={{0,3},{1,2},{2,1},{3,0},{4,7},{5,6},{6,5},{7,4},{8,11},{9,10},{10,... | collective-permute-start | bytes 2752520 | tf_op jit(solution)/shard_map/ppermute | solution.py:30
  87.0 5.1 %copy-start.2 = (f32[128,7168]{1,0:T(8,128)}, f32[128,7168]{1,0:T(8,128)S(1)}, u32[]{:S(2)}) copy-start(f32[128,7168]{1,0:T(8,128)S(1)} %fusion.41) | copy-start | bytes 11010052
  87.0 18.2 %copy-start.7 = (bf16[128,1792]{1,0:T(8,128)(2,1)S(1)}, bf16[128,1792]{1,0:T(8,128)(2,1)}, u32[]{:S(2)}) copy-start(bf16[128,1792]{1,0:T(8,128)(2,1)} %param.14) | copy-start | bytes 1376260
  89.8 2.3 collective-permute-start.14
  90.7 3.9 %collective-permute-start.13 = (bf16[128,1792]{1,0:T(8,128)(2,1)S(1)}, bf16[128,1792]{1,0:T(8,128)(2,1)S(1)}, u32[]{:S(2)}, u32[]{:S(2)}) collective-permute-start(bf16[128,1792]{1,0:T(8,128)(2,1)S(1)} %get-tuple-element.47), channel_id=1, source_target_pairs={{0,1},{1,0},{2,3},{3,2},{4,5},{5,4},{6,7},{7,6},{8,9},{9,8},{10,11... | collective-permute-start | bytes 1376264 | tf_op jit(solution)/shard_map/ppermute | solution.py:30
  92.2 13.0 %collective-permute-start.15 = (bf16[128,1792]{1,0:T(8,128)(2,1)S(1)}, bf16[128,1792]{1,0:T(8,128)(2,1)}, u32[]{:S(2)}, u32[]{:S(2)}) collective-permute-start(bf16[128,1792]{1,0:T(8,128)(2,1)S(1)} %add_convert_fusion.1), channel_id=1, source_target_pairs={{0,2},{1,3},{2,0},{3,1},{4,6},{5,7},{6,4},{7,5},{8,10},{9,11},{10,... | collective-permute-start | bytes 1376264 | tf_op jit(solution)/shard_map/ppermute | solution.py:30
  94.6 16.8 %copy-start.5 = (bf16[256,1792]{1,0:T(8,128)(2,1)S(1)}, bf16[256,1792]{1,0:T(8,128)(2,1)}, u32[]{:S(2)}) copy-start(bf16[256,1792]{1,0:T(8,128)(2,1)} %get-tuple-element.42) | copy-start | bytes 2752516
  94.6 18.5 %copy-start.12 = (s32[128,4]{0,1:T(4,128)S(1)}, s32[128,4]{0,1:T(4,128)}, u32[]{:S(2)}) copy-start(s32[128,4]{0,1:T(4,128)} %param.24) | copy-start | bytes 6148
  108.1 1.3 collective-permute-start.16
  109.4 3.7 %collective-permute-start.17 = (f32[9,128]{1,0:T(8,128)S(1)}, f32[9,128]{1,0:T(8,128)S(1)}, u32[]{:S(2)}, u32[]{:S(2)}) collective-permute-start(f32[9,128]{1,0:T(8,128)S(1)} %fusion.36), channel_id=1, source_target_pairs={{0,2},{1,3},{2,0},{3,1},{4,6},{5,7},{6,4},{7,5},{8,10},{9,11},{10,... | collective-permute-start | bytes 13832 | tf_op jit(solution)/shard_map/ppermute | solution.py:30
  110.9 22.4 %collective-permute-start.18 = (bf16[256,1792]{1,0:T(8,128)(2,1)}, bf16[256,1792]{1,0:T(8,128)(2,1)}, u32[]{:S(2)}, u32[]{:S(2)}) collective-permute-start(bf16[256,1792]{1,0:T(8,128)(2,1)} %get-tuple-element.41), channel_id=1, source_target_pairs={{0,2},{1,3},{2,0},{3,1},{4,6},{5,7},{6,4},{7,5},{8,10},{9,11},{10,... | collective-permute-start | bytes 2752520 | tf_op jit(solution)/shard_map/ppermute | solution.py:30
  111.4 22.0 %collective-permute-start.19 = (bf16[256,1792]{1,0:T(8,128)(2,1)S(1)}, bf16[256,1792]{1,0:T(8,128)(2,1)}, u32[]{:S(2)}, u32[]{:S(2)}) collective-permute-start(bf16[256,1792]{1,0:T(8,128)(2,1)S(1)} %copy-done.5), channel_id=1, source_target_pairs={{0,1},{1,0},{2,3},{3,2},{4,5},{5,4},{6,7},{7,6},{8,9},{9,8},{10,11... | collective-permute-start | bytes 2752520 | tf_op jit(solution)/shard_map/ppermute | solution.py:30
  133.4 123.7 %copy-start.1 = (bf16[16,128,512]{2,1,0:T(8,128)(2,1)S(1)}, bf16[16,128,512]{2,1,0:T(8,128)(2,1)}, u32[]{:S(2)}) copy-start(bf16[16,128,512]{2,1,0:T(8,128)(2,1)} %param.19) | copy-start | bytes 6291460
